TPU v7x, 32 devices: a whole 2x2x4 slice. The times are simulated.
32 devices in a mesh: sent: 32 (over z, y, x, core).
Axes of the slice: x: 2, y: 2, z: 4, core: 2. Of those that a mesh axis runs over, the one named last changes fastest.
Arguments:
- embeddings: bfloat16 [8192, 768], P('sent'), may hold values from -6 to 6
- cotangent: bfloat16 [2, 8192, 768], P(None, 'sent'), may hold values from -0.011962891 to 0.011962891
- drop_masks: int32 [2, 3, 8192, 768], P(None, None, 'sent'), may hold values 0 or 1
- lengths: int32 [256], P('sent'), may hold values from 0 to 128, as said below
- buckets: int32 [32], replicated, may hold values from 0 to 2, as said below
- attn_params: float32 [2463744], P('sent'), may hold values from -3 to 3
- attn_moment: float32 [2463744], P('sent'), may hold values from -1 to 1
- attn_second: float32 [2463744], P('sent'), may hold values from 0 to 1, as said below
- attn_ema: float32 [2463744], P('sent'), may hold values from -3 to 3
- head_params: float32 [5314560], P('sent'), may hold values from -3 to 3
- head_moment: float32 [5314560], P('sent'), may hold values from -1 to 1
- head_second: float32 [5314560], P('sent'), may hold values from 0 to 1, as said below
- head_ema: float32 [5314560], P('sent'), may hold values from -3 to 3
Outputs:
- hidden: bfloat16 [2, 8192, 768], P(None, 'sent')
- input_grad: float32 [8192, 768], P('sent')
- loss: float32 [], replicated
- grad_norm: float32 [], replicated
- attn_first: float32 [2463744], P('sent')
- attn_second_new: float32 [2463744], P('sent')
- attn_updated: float32 [2463744], P('sent')
- attn_average: float32 [2463744], P('sent')
- head_first: float32 [5314560], P('sent')
- head_second_new: float32 [5314560], P('sent')
- head_updated: float32 [5314560], P('sent')
- head_average: float32 [5314560], P('sent')
Inputs may be any that keep to these rules, and one draw needn't show every extreme that they name: `buckets`: sentences of device b have 32 * 2^code rows; some device has code 2. `lengths`: slot s of a device holds a sentence of 1 to its bucket length rows when s < 256 // (bucket length), else 0; the first slot of every device is full. `attn_second`: positive. `head_second`: positive.
All inputs are finite; a program needn't handle non-finite values. No bound on the sum of `drop_masks` on one device may be relied on, other than what follows from the above.
Results may differ from a plain program's by a relative error of at most 0.017.
The roundings to bfloat16 on the way count: a program that leaves them out, or rounds other values in their place, can miss the bound.
Values may be sent and summed in bfloat16 or wider, within the bound.
No kernel may reach another device: no remote copies, remote signals or barrier semaphores. Data moves between devices by JAX's collectives and lax.ppermute only.
A program may use at most 192 MiB of HBM per device.

v0:
```python
import jax
import jax.numpy as jnp
from jax import lax
from jax.sharding import PartitionSpec as P

D = 768
H = 12
HD = 64
LMIN = 32
POS = 128
STEP = 5


logit_divisor = 0.05
keep_prob = 0.9
norm_eps = 1e-06
clip_bound = 0.001
beta_first = 0.5
beta_second = 0.5
learn_rate = 0.05
decay_rate = 0.01
adam_eps = 1e-08
ema_rate = 0.8
masked_scores = -1e30
highest = lax.Precision.HIGHEST


def layer_norm(tensor, gain_vec, shift_vec):
    center = tensor - jnp.mean(tensor, axis=-1, keepdims=True)
    spread = jnp.mean(center * center, axis=-1, keepdims=True)
    return center * lax.rsqrt(spread + norm_eps) * gain_vec + shift_vec


def gelu_exact(tensor):
    return 0.5 * tensor * (1.0 + jax.scipy.special.erf(tensor * 0.7071067811865476))


def unit_scale(tensor):
    return tensor * lax.rsqrt(jnp.sum(tensor * tensor, axis=-1, keepdims=True) + norm_eps)


def bucket_length(bucket_code):
    return (LMIN * jnp.where(bucket_code == 0, 1, jnp.where(bucket_code == 1, 2, 4))).astype(
        jnp.int32
    )


def plain_dot(left_op, right_op):
    return jnp.dot(left_op, right_op, preferred_element_type=jnp.float32)


def rows_dot(left_op, right_op):
    return lax.dot_general(
        left_op, right_op, (((0,), (0,)), ((), ())), preferred_element_type=jnp.float32
    )


def target_dot_terms(left_op, right_op):
    return lax.dot_general(
        left_op, right_op, (((1,), (1,)), ((), ())), preferred_element_type=jnp.float32
    )


def adam_step(grad_flat, params, moment, second, average):
    first_new = beta_first * moment + (1.0 - beta_first) * grad_flat
    second_new = beta_second * second + (1.0 - beta_second) * grad_flat * grad_flat
    fix_first = 1.0 - beta_first**STEP
    fix_second = 1.0 - beta_second**STEP
    adam_dir = first_new / fix_first / (jnp.sqrt(second_new / fix_second) + adam_eps)
    updated = params - learn_rate * (adam_dir + decay_rate * params)
    average_new = ema_rate * average + (1.0 - ema_rate) * updated
    return (first_new, second_new, updated, average_new)


def on_device(
    embeddings,
    cotangent,
    drop_masks,
    lengths,
    buckets,
    attn_params,
    attn_moment,
    attn_second,
    attn_ema,
    head_params,
    head_moment,
    head_second,
    head_ema,
):
    tok_rows = embeddings.shape[0]
    slot_count = lengths.shape[0]
    all_rows = 2 * tok_rows
    device = lax.axis_index("sent")
    attn_full, head_full = (
        lax.all_gather(attn_params.astype(jnp.bfloat16), "sent", axis=0, tiled=True),
        lax.all_gather(head_params.astype(jnp.bfloat16), "sent", axis=0, tiled=True),
    )
    attn_mats = attn_full[: 4 * D * D].reshape(D, 4 * D)
    attn_vecs_low = attn_full[4 * D * D :].reshape(D, 8 + POS)
    attn_vecs = attn_vecs_low.astype(jnp.float32)
    head_mats = head_full[: 9 * D * D].reshape(D, 9 * D)
    head_vecs = head_full[9 * D * D :].reshape(D, 8).astype(jnp.float32)
    w_qkv = attn_mats[:, : 3 * D]
    w_out = attn_mats[:, 3 * D :]
    w_up = head_mats[:, : 4 * D]
    w_down = head_mats[:, 4 * D : 8 * D]
    w_pool = head_mats[:, 8 * D :]
    bucket_all = bucket_length(buckets)
    slot_ids = jnp.arange(slot_count, dtype=jnp.int32)
    valid_everything = (
        (slot_ids[None, :] < (tok_rows // bucket_all)[:, None]).astype(jnp.float32).reshape(-1)
    )
    bucket_len = bucket_all[device]
    sent_count = tok_rows // bucket_len
    valid_own = (slot_ids < sent_count).astype(jnp.float32)
    row_ids = jnp.arange(tok_rows, dtype=jnp.int32)
    sentence = row_ids // bucket_len
    row_place = row_ids % bucket_len
    slot_len = jnp.sum(
        jnp.where(sentence[:, None] == slot_ids[None, :], lengths[None, :], 0), axis=1
    )
    key_ok = row_place < slot_len
    block = POS
    sent_blocks = sentence.reshape(-1, block)
    ok_blocks = key_ok.reshape(-1, block)
    allowed = (sent_blocks[:, :, None] == sent_blocks[:, None, :]) & ok_blocks[:, None, :]
    allowed = jnp.concatenate([allowed, allowed], axis=0)[:, None]
    place_hot = (row_place[:, None] == jnp.arange(POS, dtype=jnp.int32)[None, :]).astype(
        jnp.bfloat16
    )
    pos_rows = plain_dot(place_hot, attn_vecs_low[:, 8:].T)
    emb_rows = embeddings.astype(jnp.float32) + pos_rows + attn_vecs[:, 7]
    normed, emb_back = jax.vjp(layer_norm, emb_rows, attn_vecs[:, 5], attn_vecs[:, 6])
    keep_masks = drop_masks.astype(jnp.float32) / keep_prob
    keep_attn = keep_masks[:, 1].reshape(all_rows, D)
    keep_ffn = keep_masks[:, 2].reshape(all_rows, D)
    attn_in = (normed[None] * keep_masks[:, 0]).reshape(all_rows, D)
    attn_in_low = attn_in.astype(jnp.bfloat16)
    qkv_bias = jnp.concatenate([attn_vecs[:, 0], jnp.zeros((D,), jnp.float32), attn_vecs[:, 1]])
    qkv_low = (plain_dot(attn_in_low, w_qkv) + qkv_bias).astype(jnp.bfloat16)
    head_split = qkv_low.reshape(-1, block, 3, H, HD)
    queries = head_split[:, :, 0]
    keys_low = head_split[:, :, 1]
    values_low = head_split[:, :, 2]
    score_scale = HD ** (-0.5)
    raw_scores = jnp.einsum(
        "bqhd,bkhd->bhqk", queries, keys_low, preferred_element_type=jnp.float32
    )
    scores = jnp.where(allowed, raw_scores * score_scale, masked_scores)
    row_top = jnp.max(scores, axis=-1, keepdims=True)
    expo_vals = jnp.exp(scores - row_top)
    row_total = jnp.sum(expo_vals, axis=-1, keepdims=True)
    attn_probs = expo_vals / row_total
    score_lse = row_top + jnp.log(row_total)
    mixed_out = jnp.einsum(
        "bhqk,bkhd->bqhd",
        attn_probs.astype(jnp.bfloat16),
        values_low,
        preferred_element_type=jnp.float32,
    )
    mixed_low = mixed_out.reshape(all_rows, D).astype(jnp.bfloat16)
    branch = plain_dot(mixed_low, w_out) + attn_vecs[:, 2]
    first_res = attn_in + keep_attn * branch
    first_norm, first_back = jax.vjp(layer_norm, first_res, attn_vecs[:, 3], attn_vecs[:, 4])
    first_low = first_norm.astype(jnp.bfloat16)
    up_bias = head_vecs[:, :4].T.reshape(4 * D)
    up_pre = plain_dot(first_low, w_up) + up_bias
    active, gelu_back = jax.vjp(gelu_exact, up_pre)
    active_low = active.astype(jnp.bfloat16)
    down_out = target_dot_terms(active_low, w_down) + head_vecs[:, 4]
    second_res = first_norm + keep_ffn * down_out
    second_norm, second_back = jax.vjp(layer_norm, second_res, head_vecs[:, 5], head_vecs[:, 6])
    hidden_out = second_norm.astype(jnp.bfloat16).reshape(2, tok_rows, D)
    cls_pick = jnp.minimum(slot_ids, sent_count - 1) * bucket_len
    cls_rows = jnp.take(second_norm.reshape(2, tok_rows, D), cls_pick, axis=1).reshape(
        2 * slot_count, D
    )
    cls_low = cls_rows.astype(jnp.bfloat16)
    pooled = jnp.tanh(plain_dot(cls_low, w_pool) + head_vecs[:, 7])
    unit_rows, unit_back = jax.vjp(unit_scale, pooled)
    unit_low = unit_rows.astype(jnp.bfloat16)
    query_embeddings = unit_low[:slot_count]
    positive_view_set = unit_low[slot_count:]
    target_sentence_set, everyone = (
        lax.all_gather(positive_view_set, "sent", axis=0, tiled=True),
        lax.all_gather(query_embeddings, "sent", axis=0, tiled=True),
    )
    own_cols = device * slot_count + slot_ids
    col_ids = jnp.arange(target_sentence_set.shape[0], dtype=jnp.int32)
    pos_hot = col_ids[None, :] == own_cols[:, None]
    cosine_logit_table = jnp.where(
        valid_everything[None, :] > 0,
        target_dot_terms(query_embeddings, target_sentence_set) / logit_divisor,
        masked_scores,
    )
    sim_top = jnp.max(cosine_logit_table, axis=-1, keepdims=True)
    row_lse = sim_top[:, 0] + jnp.log(jnp.sum(jnp.exp(cosine_logit_table - sim_top), axis=-1))
    positive = jnp.sum(jnp.where(pos_hot, cosine_logit_table, 0.0), axis=-1)
    local_loss = jnp.sum(valid_own * (row_lse - positive))
    loss_sum = lax.psum(local_loss, "sent")
    cosine_logit_cotangent = valid_own[:, None] * (
        jnp.exp(cosine_logit_table - row_lse[:, None]) - pos_hot.astype(jnp.float32)
    )
    cosine_logit_summed = (cosine_logit_cotangent / logit_divisor).astype(jnp.bfloat16)
    d_anchor = plain_dot(cosine_logit_summed, target_sentence_set)
    all_lse = lax.all_gather(row_lse, "sent", axis=0, tiled=True)
    back_sim = target_dot_terms(everyone, positive_view_set) / logit_divisor
    back_hot = (col_ids[:, None] == own_cols[None, :]).astype(jnp.float32)
    back_grad = valid_everything[:, None] * (
        jnp.exp(back_sim - all_lse[:, None]) * valid_own[None, :] - back_hot
    )
    d_partner = rows_dot((back_grad / logit_divisor).astype(jnp.bfloat16), everyone)
    d_unit = jnp.concatenate([d_anchor, d_partner], axis=0)
    d_pooled = unit_back(d_unit)[0]
    d_pool_pre = d_pooled * (1.0 - pooled * pooled)
    pool_low = d_pool_pre.astype(jnp.bfloat16)
    g_pool = rows_dot(cls_low, pool_low)
    g_pool_bias = jnp.sum(d_pool_pre, axis=0)
    d_cls = target_dot_terms(pool_low, w_pool).reshape(2, slot_count, D)
    pick_hot = ((row_ids[None, :] == cls_pick[:, None]) & (slot_ids[:, None] < sent_count)).astype(
        jnp.float32
    )
    d_second = cotangent.astype(jnp.float32) + jnp.einsum(
        "st,vsd->vtd", pick_hot, d_cls, precision=highest
    )
    d_second_res, g_gain_two, g_shift_two = second_back(d_second.reshape(all_rows, D))
    d_down = d_second_res * keep_ffn
    g_down_bias = jnp.sum(d_down, axis=0)
    down_low = d_down.astype(jnp.bfloat16)
    g_down = rows_dot(down_low, active_low)
    d_active = plain_dot(down_low, w_down)
    d_up = gelu_back(d_active)[0]
    g_up_bias = jnp.sum(d_up, axis=0)
    up_low = d_up.astype(jnp.bfloat16)
    g_up = rows_dot(first_low, up_low)
    d_first = d_second_res + target_dot_terms(up_low, w_up)
    head_vec_grad = jnp.concatenate(
        [
            g_up_bias.reshape(4, D).T,
            jnp.stack([g_down_bias, g_gain_two, g_shift_two, g_pool_bias], axis=1),
        ],
        axis=1,
    )
    head_grad = jnp.concatenate(
        [jnp.concatenate([g_up, g_down, g_pool], axis=1).reshape(-1), head_vec_grad.reshape(-1)]
    )
    d_first_res, g_gain_one, g_shift_one = first_back(d_first)
    d_branch = d_first_res * keep_attn
    g_out_bias = jnp.sum(d_branch, axis=0)
    branch_low = d_branch.astype(jnp.bfloat16)
    g_out = rows_dot(mixed_low, branch_low)
    d_mixed = target_dot_terms(branch_low, w_out).astype(jnp.bfloat16).reshape(-1, block, H, HD)
    again = jnp.where(
        allowed,
        jnp.einsum("bqhd,bkhd->bhqk", queries, keys_low, preferred_element_type=jnp.float32)
        * score_scale,
        masked_scores,
    )
    probs_again = jnp.exp(again - score_lse)
    d_values = jnp.einsum(
        "bhqk,bqhd->bkhd",
        probs_again.astype(jnp.bfloat16),
        d_mixed,
        preferred_element_type=jnp.float32,
    )
    d_probs = jnp.einsum("bqhd,bkhd->bhqk", d_mixed, values_low, preferred_element_type=jnp.float32)
    row_delta = jnp.sum(probs_again * d_probs, axis=-1, keepdims=True)
    score_low = (probs_again * (d_probs - row_delta) * score_scale).astype(jnp.bfloat16)
    d_queries = jnp.einsum(
        "bhqk,bkhd->bqhd", score_low, keys_low, preferred_element_type=jnp.float32
    )
    d_keys = jnp.einsum("bhqk,bqhd->bkhd", score_low, queries, preferred_element_type=jnp.float32)
    d_qkv = jnp.stack([d_queries, d_keys, d_values], axis=2).reshape(all_rows, 3 * D)
    g_q_bias = jnp.sum(d_queries.reshape(all_rows, D), axis=0)
    g_v_bias = jnp.sum(d_values.reshape(all_rows, D), axis=0)
    qkv_grad_low = d_qkv.astype(jnp.bfloat16)
    g_qkv = rows_dot(attn_in_low, qkv_grad_low)
    d_attn_in = d_first_res + target_dot_terms(qkv_grad_low, w_qkv)
    d_normed = jnp.sum(d_attn_in.reshape(2, tok_rows, D) * keep_masks[:, 0], axis=0)
    input_grad, g_gain_emb, g_shift_emb = emb_back(d_normed)
    g_type = jnp.sum(input_grad, axis=0)
    g_table = lax.dot_general(
        place_hot.astype(jnp.float32),
        input_grad,
        (((0,), (0,)), ((), ())),
        precision=highest,
        preferred_element_type=jnp.float32,
    )
    attn_vec_grad = jnp.concatenate(
        [
            jnp.stack(
                [
                    g_q_bias,
                    g_v_bias,
                    g_out_bias,
                    g_gain_one,
                    g_shift_one,
                    g_gain_emb,
                    g_shift_emb,
                    g_type,
                ],
                axis=1,
            ),
            g_table.T,
        ],
        axis=1,
    )
    attn_grad = jnp.concatenate(
        [jnp.concatenate([g_qkv, g_out], axis=1).reshape(-1), attn_vec_grad.reshape(-1)]
    )
    attn_share, head_share = (
        lax.psum_scatter(attn_grad, "sent", scatter_dimension=0, tiled=True),
        lax.psum_scatter(head_grad, "sent", scatter_dimension=0, tiled=True),
    )
    squares = jnp.sum(attn_share * attn_share) + jnp.sum(head_share * head_share)
    total_squares = lax.psum(squares, "sent")
    loss = loss_sum / jnp.sum(valid_everything)
    grad_norm = jnp.sqrt(total_squares)
    clip_scale = jnp.minimum(1.0, clip_bound / grad_norm)
    attn_new = adam_step(attn_share * clip_scale, attn_params, attn_moment, attn_second, attn_ema)
    head_new = adam_step(head_share * clip_scale, head_params, head_moment, head_second, head_ema)
    return (
        hidden_out,
        input_grad,
        loss,
        grad_norm,
        attn_new[0],
        attn_new[1],
        attn_new[2],
        attn_new[3],
        head_new[0],
        head_new[1],
        head_new[2],
        head_new[3],
    )


def solution(mesh):
    in_specs = (
        P("sent", None),
        P(None, "sent", None),
        P(None, None, "sent", None),
        P("sent"),
        P(),
        P("sent"),
        P("sent"),
        P("sent"),
        P("sent"),
        P("sent"),
        P("sent"),
        P("sent"),
        P("sent"),
    )
    out_specs = (
        P(None, "sent", None),
        P("sent", None),
        P(),
        P(),
        P("sent"),
        P("sent"),
        P("sent"),
        P("sent"),
        P("sent"),
        P("sent"),
        P("sent"),
        P("sent"),
    )
    return jax.shard_map(
        on_device, mesh=mesh, in_specs=in_specs, out_specs=out_specs, check_vma=False
    )
```

profile of v0, /device:TPU:0, one launch (start us, length us, event | category | flops | bytes accessed | tf_op | source)
XLA Modules:
  0.0 1196.5 jit_solution(9172695935254159472)
XLA Ops:
  7.2 1.1 convert_element_type.158
  8.4 1.0 convert_element_type.148
  9.4 4.7 broadcast.441
  14.0 6.1 dynamic-update-slice.1
  20.2 2.6 broadcast.440
  22.8 3.2 dynamic-update-slice
  34.3 3.1 convert_multiply_fusion
  37.5 2.1 copy-done
  39.6 2.1 fusion.155
  41.7 252.7 %all-reduce.13.cloned.1.call-done = (bf16[5314560]{0:T(1024)(128)(2,1)}, bf16[2463744]{0:T(1024)(128)(2,1)}) async-done(((bf16[5314560]{0:T(1024)(128)(2,1)}, bf16[2463744]{0:T(1024)(128)(2,1)}), (bf16[5314560]{0:T(1024)(128)(2,1)}, bf16[2463744]{0:T(1024)(128)(2,1)})) %all-reduce.13.cloned.1.call-update) | async-done | bytes 15556624
  295.2 9.6 slice.165
  304.8 2.7 slice.153
  307.7 1.1 reshape.422
  308.9 2.4 slice_reduce_fusion
  311.5 19.7 %reshape.424 = bf16[768,6912]{1,0:T(8,128)(2,1)} reshape(bf16[5308416]{0:T(1024)(128)(2,1)} %slice.165) | data formatting | bytes 21233664 | tf_op jit(solution)/shard_map/reshape | solution.py:101
  331.9 8.2 slice.120
  340.3 0.9 copy-done.10
  341.2 3.4 fusion.53
  344.6 3.4 fusion.1
  348.0 4.3 copy.94
  352.3 5.5 reshape.423
  357.7 2.6 fusion.156
  360.4 0.8 fusion.159
  363.7 3.2 fusion.160
  367.7 5.0 multiply_convert_fusion
  372.7 2.9 fusion.161
  376.2 0.9 copy-done.25
  378.5 1.7 multiply_reduce_fusion.12
  380.3 41.0 %all_gather.18 = bf16[256,768]{1,0:T(8,128)(2,1)S(1)} all-gather(bf16[8,768]{1,0:T(8,128)(2,1)S(1)} %get-tuple-element.78), channel_id=1, replica_groups=mesh['sent'=32] {'sent'}, dimensions={0}, use_global_device_ids=true | all-gather | bytes 405504 | tf_op jit(solution)/shard_map/all_gather | solution.py:186
  421.3 37.7 %all_gather.17 = bf16[256,768]{1,0:T(8,128)(2,1)S(1)} all-gather(bf16[8,768]{1,0:T(8,128)(2,1)S(1)} %get-tuple-element.77), channel_id=1, replica_groups=mesh['sent'=32] {'sent'}, dimensions={0}, use_global_device_ids=true | all-gather | bytes 405504 | tf_op jit(solution)/shard_map/all_gather | solution.py:185
  460.4 37.4 %all-reduce.2 = f32[256]{0:T(256)S(1)} all-reduce(f32[256]{0:T(256)S(1)} %dynamic-update-slice.2), channel_id=1, replica_groups=mesh['sent'=32] {'sent'}, use_global_device_ids=true, to_apply=%add.2 | all-reduce | flops 256 | bytes 2048
  498.7 1.7 convolution_bitcast_fusion
  500.4 2.2 fusion.166
  504.9 8.0 fusion.165
  512.9 6.6 multiply_reduce_fusion.1
  521.4 0.9 copy-done.29
  522.3 2.1 convolution_convert_fusion
  524.4 1.2 copy.103
  525.6 1.9 reshape.429
  527.5 3.5 fusion.85
  531.0 2.1 bitcast_reduce_fusion
  533.2 7.3 fusion.50
  540.5 7.4 bitcast_reduce_fusion.1
  547.9 3.5 fusion.82
  551.3 1.9 fusion.104
  553.3 5.3 fusion.93
  558.6 5.5 fusion.44
  564.4 2.3 copy.109
  566.7 2.2 fusion.38
  568.9 2.7 fusion.34
  573.8 1.5 reshape.432
  575.3 6.8 fusion.26
  582.1 7.9 maximum_bitcast_fusion
  590.1 9.7 copy.125
  600.2 14.2 %pad_maximum_fusion.1 = f32[768,6912]{1,0:T(8,128)} fusion(f32[768,768]{1,0:T(8,128)S(1)} %copy-done.8, f32[768,3072]{1,0:T(8,128)} %fusion.93, f32[768,3072]{1,0:T(8,128)} %fusion.44), kind=kLoop, calls=%fused_computation.3 | loop fusion | flops 10616832 | bytes 42467328 | tf_op jit(solution)/shard_map/concatenate | solution.py:245
  614.4 22.2 %reshape.433 = f32[5308416]{0:T(1024)} reshape(f32[768,6912]{1,0:T(8,128)} %pad_maximum_fusion.1) | data formatting | bytes 42467328 | tf_op jit(solution)/shard_map/reshape | solution.py:245
  636.6 9.7 pad_maximum_fusion.2
  646.4 17.5 %pad_maximum_fusion = f32[5314560]{0:T(1024)} fusion(f32[6144]{0:T(1024)S(1)} %reshape.435, f32[5308416]{0:T(1024)} %reshape.433), kind=kLoop, calls=%fused_computation.2 | loop fusion | flops 5314560 | bytes 42516480 | tf_op jit(solution)/shard_map/concatenate | solution.py:244
  665.2 469.0 %all-reduce.11.cloned.1.call-done = (f32[2463744]{0:T(1024)}, f32[5314560]{0:T(1024)}) async-done(((f32[2463744]{0:T(1024)}, f32[5314560]{0:T(1024)}), (f32[2463744]{0:T(1024)}, f32[5314560]{0:T(1024)})) %all-reduce.11.cloned.1.call-update) | async-done | bytes 31113232
  1134.2 1.7 multiply_reduce_fusion.10
  1135.9 1.9 multiply_reduce_fusion.9
  1139.2 39.9 %all-reduce.5 = (f32[]{:T(128)}, f32[]{:T(128)}) all-reduce(f32[]{:T(128)} %get-tuple-element.55, f32[]{:T(128)S(6)} %add.348), channel_id=1, replica_groups=mesh['sent'=32] {'sent'}, use_global_device_ids=true, to_apply=%region_23.24 | all-reduce | flops 2 | bytes 16 | tf_op jit(solution)/shard_map/psum | solution.py:200
  1181.2 2.5 multiply_add_fusion.7
  1183.8 3.3 multiply_add_fusion.5
  (206 shorter events, 22.8 us)
Async XLA Ops:
  7.2 287.3 %all-reduce.13.cloned.1.call-start = ((), (), s32[]{:S(2)}) async-start(), calls=%async_computation.1 | async-start | bytes 31113216
  26.0 0.7 copy-start.47
  26.0 8.0 copy-start.44
  26.0 1108.2 %all-reduce.11.cloned.1.call-start = ((), (), s32[]{:S(2)}) async-start(), calls=%async_computation | async-start | bytes 62226432
  26.8 5.4 copy-start.45
  37.5 2.2 copy-start
  41.7 321.8 %copy-start.1 = (f32[2,1,256,768]{3,2,1,0:T(8,128)}, f32[2,1,256,768]{3,2,1,0:T(8,128)S(1)}, u32[]{:S(2)}) copy-start(f32[2,1,256,768]{3,2,1,0:T(8,128)S(1)} %get-tuple-element.69) | copy-start | bytes 4718596
  295.2 9.6 copy-start.20
  311.5 19.7 %copy-start.42 = (bf16[256,768]{1,0:T(8,128)(2,1)S(1)}, bf16[256,768]{1,0:T(8,128)(2,1)}, u32[]{:S(2)}) copy-start(bf16[256,768]{1,0:T(8,128)(2,1)} %param.13) | copy-start | bytes 1179652
  340.1 4.5 copy-start.9
  340.3 0.9 copy-start.10
  360.4 1.6 copy-start.34
  360.4 1.6 copy-start.35
  360.4 1.7 copy-start.21
  361.2 1.7 copy-start.5
  362.0 1.7 copy-start.19
  362.1 5.2 slice-start
  362.1 5.2 slice-start.1
  363.5 3.4 copy-start.12
  363.7 3.9 slice-start.2
  366.9 5.7 copy-start.3
  367.6 5.0 copy-start.15
  372.6 2.9 copy-start.26
  376.2 0.9 copy-start.25
  503.2 1.4 copy-start.16
  504.9 8.0 copy-start.23
  504.9 8.0 copy-start.4
  512.9 6.7 copy-start.48
  519.6 1.4 copy-start.2
  520.2 1.2 copy-start.17
  521.4 0.9 copy-start.29
  527.5 3.6 copy-start.6
  540.5 7.4 copy-start.13
  547.9 5.4 copy-start.24
  547.9 5.4 copy-start.27
  553.3 5.3 copy-start.49
  553.3 13.3 %slice-start.3 = ((s8[4718592]{0:T(1024)(128)(4,1)}), s8[4194304]{0:T(1024)(128)(4,1)S(1)}, s32[]{:S(2)}) async-start(s8[4718592]{0:T(1024)(128)(4,1)} %bitcast.154), calls=%async_computation.5 | async-start | bytes 8388608
  558.6 5.5 copy-start.22
  558.6 5.5 copy-start.36
  558.6 5.5 copy-start.37
  558.6 8.1 slice-start.4
  564.3 2.3 copy-start.14
  564.3 2.3 copy-start.18
  566.6 2.3 copy-start.31
  566.7 2.2 copy-start.11
  572.3 3.1 copy-start.38
  572.6 9.5 copy-start.28
  575.3 6.8 copy-start.7
  590.1 10.1 copy-start.8
  614.4 22.2 %copy-start.32 = (f32[104448]{0:T(1024)S(1)}, f32[104448]{0:T(1024)}, u32[]{:S(2)}) copy-start(f32[104448]{0:T(1024)} %reshape.432) | copy-start | bytes 1253380
  663.9 0.7 copy-start.46
  663.9 517.3 %copy-start.33 = (f32[76992]{0:T(1024)S(1)}, f32[76992]{0:T(1024)}, u32[]{:S(2)}) copy-start(f32[76992]{0:T(1024)} %param.18) | copy-start | bytes 923908
  663.9 517.3 %copy-start.43 = (f32[76992]{0:T(1024)S(1)}, f32[76992]{0:T(1024)}, u32[]{:S(2)}) copy-start(f32[76992]{0:T(1024)} %param.21) | copy-start | bytes 923908
  663.9 519.8 %copy-start.30 = (f32[166080]{0:T(1024)S(1)}, f32[166080]{0:T(1024)}, u32[]{:S(2)}) copy-start(f32[166080]{0:T(1024)} %param.22) | copy-start | bytes 1992964
  663.9 519.8 %copy-start.39 = (f32[166080]{0:T(1024)S(1)}, f32[166080]{0:T(1024)}, u32[]{:S(2)}) copy-start(f32[166080]{0:T(1024)} %param.25) | copy-start | bytes 1992964
  663.9 519.8 %copy-start.40 = (f32[166080]{0:T(1024)S(1)}, f32[166080]{0:T(1024)}, u32[]{:S(2)}) copy-start(f32[166080]{0:T(1024)} %param.24) | copy-start | bytes 1992964
  663.9 519.8 %copy-start.41 = (f32[166080]{0:T(1024)S(1)}, f32[166080]{0:T(1024)}, u32[]{:S(2)}) copy-start(f32[166080]{0:T(1024)} %param.23) | copy-start | bytes 1992964
Sparse Core Ops, SparseCore 0:
  26.1 268.3 all-reduce.12
  664.0 470.1 all-reduce.10
where the time goes:
time: 1210 us; the launch traced here: 1200 us
  waiting for transfers between devices  722 us (60%)
  blocking collectives  156 us (13%)
  local copies, waits for them, and re-layouts  127 us (10%)
  matrix products  85.7 us (7%)
  other arithmetic  82 us (7%)
  between operations  24.3 us (2%)
    unnamed x4, waiting for transfers between devices  722 us
    all_gather x1, blocking collectives, on_device(): lax.all_gather(query_embeddings, 'sent', axis=0, tiled=True)  41 us
    psum x1, blocking collectives, on_device(): loss_sum = lax.psum(local_loss, 'sent')  39.9 us
    all_gather x1, blocking collectives, on_device(): lax.all_gather(positive_view_set, 'sent', axis=0, tiled=True)  37.7 us
    unnamed x1, blocking collectives  37.4 us
    unnamed x116, local copies, waits for them, and re-layouts  34.9 us
  transfers between devices with their start and end apart: 2, of which 2 were waited for; matrix products, arithmetic and copies ran while one was open for 1% of the time, Pallas kernels for 0%

commit v1 on v0

--- a/solution.py
+++ b/solution.py
@@ -1,6 +1,10 @@
+import functools
+
 import jax
 import jax.numpy as jnp
 from jax import lax
+from jax.experimental import pallas as pl
+from jax.experimental.pallas import tpu as pltpu
 from jax.sharding import PartitionSpec as P
 
 D = 768
@@ -70,6 +74,252 @@
     updated = params - learn_rate * (adam_dir + decay_rate * params)
     average_new = ema_rate * average + (1.0 - ema_rate) * updated
     return (first_new, second_new, updated, average_new)
+
+
+LANES = 128
+VMEM_CAP = 60 * 2**20
+CORE, XBIT, YBIT, ZBITS = 1, 2, 4, (8, 16, 24)
+
+
+def swap(value, bit):
+    count = lax.axis_size("sent")
+    return lax.ppermute(value, "sent", [(i, i ^ bit) for i in range(count)])
+
+
+def is_grid(count, *shards):
+    return count == 32 and all(2 * shard % LANES == 0 for shard in shards)
+
+
+def block_rows(shard):
+    return -(-(-(-shard // LANES) + 8) // 16) * 16
+
+
+def first_row(device, shard):
+    return (device * shard) // LANES
+
+
+def pack_shard(values, device):
+    shard = values.shape[0]
+    rows = block_rows(shard)
+    size = rows * LANES
+    odd = (device * shard) % LANES != 0
+    lead = jnp.where(
+        odd,
+        jnp.pad(values, (LANES // 2, size - shard - LANES // 2)),
+        jnp.pad(values, (0, size - shard)),
+    ).reshape(rows, LANES)
+    offset = first_row(device, shard) % 8
+    padded = jnp.pad(lead, ((8, 0), (0, 0)))
+    return lax.dynamic_slice(padded, (8 - offset, 0), (rows, LANES)).astype(jnp.bfloat16)
+
+
+def unpack_shard(block, device, shard):
+    rows = -(-shard // LANES)
+    offset = first_row(device, shard) % 8
+    odd = (device * shard) % LANES != 0
+    flat = lax.dynamic_slice(block, (offset, 0), (rows, LANES)).reshape(-1)
+    longer = jnp.pad(flat, (0, LANES))
+    return jnp.where(odd, longer[LANES // 2 : LANES // 2 + shard], flat[:shard])
+
+
+def piece_slots(me):
+    order = []
+    for core in (0, 1):
+        order += [
+            (core, 0, 0, 0, 4),
+            (core, 0, 1, 0, 2),
+            (core, 0, 1, 2, 2),
+            (core, 1, 0, 0, 2),
+            (core, 1, 0, 2, 2),
+            (core, 1, 1, 0, 2),
+            (core, 1, 1, 2, 2),
+        ]
+    slots = []
+    for core, y, x, z, n in order:
+        slots.append([me ^ (core + 2 * x + 4 * y + 8 * (z + k)) for k in range(n)])
+    return slots
+
+
+def gather_pieces(block):
+    zs = [block] + [swap(block, bit) for bit in ZBITS]
+    low_half = jnp.stack(zs[:2])
+    high_half = jnp.stack(zs[2:])
+    x_low, x_high = swap(low_half, XBIT), swap(high_half, XBIT)
+    y_low, y_high = swap(low_half, YBIT), swap(high_half, YBIT)
+    d_low, d_high = swap(y_low, XBIT), swap(x_high, YBIT)
+    own = [jnp.concatenate([low_half, high_half]), x_low, x_high, y_low, y_high, d_low, d_high]
+    return own + [swap(piece, CORE) for piece in own]
+
+
+def low_sum(*terms):
+    total = terms[0].astype(jnp.float32)
+    for term in terms[1:]:
+        total = total + term.astype(jnp.float32)
+    return total.astype(jnp.bfloat16)
+
+
+def scatter_pieces(pieces):
+    got = [swap(piece, CORE) for piece in pieces[7:]]
+    own, x_low, x_high, y_low, y_high, d_low, d_high = pieces[:7]
+    d_low = swap(low_sum(d_low, got[5]), XBIT)
+    d_high = swap(low_sum(d_high, got[6]), YBIT)
+    x_low = swap(low_sum(x_low, got[1]), XBIT)
+    y_high = swap(low_sum(y_high, got[4]), YBIT)
+    x_high = swap(low_sum(x_high, got[2], d_high), XBIT)
+    y_low = swap(low_sum(y_low, got[3], d_low), YBIT)
+    low_half = low_sum(own[:2], got[0][:2], x_low, y_low)
+    high_half = low_sum(own[2:], got[0][2:], x_high, y_high)
+    zs = [low_half[0], low_half[1], high_half[0], high_half[1]]
+    total = zs[0].astype(jnp.float32)
+    for value, bit in zip(zs[1:], ZBITS):
+        total = total + swap(value, bit).astype(jnp.float32)
+    return total
+
+
+def unflatten_kernel(shard, cols, me_ref, *refs):
+    pieces, (w_ref, v_ref), (stage, flat, sems) = refs[:14], refs[14:16], refs[16:]
+    count, rows = stage.shape[0], stage.shape[1]
+    me = me_ref[0]
+    for piece, slots in zip(pieces, piece_slots(me)):
+        for k, slot in enumerate(slots):
+            pltpu.make_async_copy(piece.at[k], stage.at[slot], sems.at[slot]).start()
+    flat[pl.ds(0, 8), :] = jnp.zeros((8, LANES), jnp.float32)
+
+    def place(device, carry):
+        pltpu.make_async_copy(pieces[0].at[0], stage.at[device], sems.at[device]).wait()
+        at = pl.multiple_of(device * shard // LANES // 8 * 8, 8)
+        before = flat[pl.ds(at, 8), :]
+        flat[pl.ds(at, rows), :] = stage[device].astype(jnp.float32)
+        flat[pl.ds(at, 8), :] += before
+        return carry
+
+    lax.fori_loop(0, count, place, 0)
+
+    def gather_rows(group, carry):
+        at = pl.multiple_of(group * 16, 16)
+        for col in range(cols):
+            rows16 = flat[pl.ds(group * 16 * cols + col, 16, stride=cols), :]
+            w_ref[pl.ds(at, 16), pl.ds(col * LANES, LANES)] = rows16.astype(jnp.bfloat16)
+        return carry
+
+    lax.fori_loop(0, D // 16, gather_rows, 0)
+    v_ref[...] = flat[pl.ds(D * cols, v_ref.shape[0]), :]
+
+
+def unflatten(pieces, me, shard, cols):
+    rows = pieces[0].shape[1]
+    whole = shard * 32 // LANES
+    return pl.pallas_call(
+        functools.partial(unflatten_kernel, shard, cols),
+        out_shape=(
+            jax.ShapeDtypeStruct((D, cols * LANES), jnp.bfloat16),
+            jax.ShapeDtypeStruct((whole - D * cols, LANES), jnp.float32),
+        ),
+        in_specs=[pl.BlockSpec(memory_space=pltpu.SMEM)] + [pl.BlockSpec(memory_space=pl.ANY)] * 14,
+        out_specs=(pl.BlockSpec(memory_space=pltpu.VMEM), pl.BlockSpec(memory_space=pltpu.VMEM)),
+        scratch_shapes=[
+            pltpu.VMEM((32, rows, LANES), jnp.bfloat16),
+            pltpu.VMEM((whole + rows, LANES), jnp.float32),
+            pltpu.SemaphoreType.DMA((32,)),
+        ],
+        compiler_params=pltpu.CompilerParams(vmem_limit_bytes=VMEM_CAP),
+    )(jnp.reshape(me, (1,)), *pieces)
+
+
+def flatten_kernel(shard, widths, me_ref, *refs):
+    n_in = len(widths)
+    mats, v_ref = refs[:n_in], refs[n_in]
+    pieces, (stage, flat, sems) = refs[n_in + 1 : n_in + 15], refs[n_in + 15 :]
+    count, rows = stage.shape[0], stage.shape[1]
+    cols = sum(widths)
+    me = me_ref[0]
+
+    def scatter_rows(group, carry):
+        at = pl.multiple_of(group * 16, 16)
+        col = 0
+        for mat, width in zip(mats, widths):
+            for k in range(width):
+                rows16 = mat[pl.ds(at, 16), pl.ds(k * LANES, LANES)].astype(jnp.float32)
+                flat[pl.ds(group * 16 * cols + col, 16, stride=cols), :] = rows16
+                col += 1
+        return carry
+
+    lax.fori_loop(0, D // 16, scatter_rows, 0)
+    flat[pl.ds(D * cols, v_ref.shape[0]), :] = v_ref[...]
+    tail = D * cols + v_ref.shape[0]
+    flat[pl.ds(tail, rows), :] = jnp.zeros((rows, LANES), jnp.float32)
+    copies = []
+    for piece, slots in zip(pieces, piece_slots(me)):
+        for k, slot in enumerate(slots):
+            at = pl.multiple_of(slot * shard // LANES // 8 * 8, 8)
+            stage[slot] = flat[pl.ds(at, rows), :].astype(jnp.bfloat16)
+            copy = pltpu.make_async_copy(stage.at[slot], piece.at[k], sems.at[len(copies)])
+            copy.start()
+            copies.append(copy)
+    for copy in copies:
+        copy.wait()
+
+
+def flatten(mats, vec_rows, me, shard):
+    rows = block_rows(shard)
+    whole = shard * 32 // LANES
+    widths = tuple(mat.shape[1] // LANES for mat in mats)
+    counts = [len(slots) for slots in piece_slots(0)]
+    return pl.pallas_call(
+        functools.partial(flatten_kernel, shard, widths),
+        out_shape=tuple(jax.ShapeDtypeStruct((n, rows, LANES), jnp.bfloat16) for n in counts),
+        in_specs=[pl.BlockSpec(memory_space=pltpu.SMEM)]
+        + [pl.BlockSpec(memory_space=pltpu.VMEM)] * (len(mats) + 1),
+        out_specs=tuple(pl.BlockSpec(memory_space=pl.ANY) for _ in counts),
+        scratch_shapes=[
+            pltpu.VMEM((32, rows, LANES), jnp.bfloat16),
+            pltpu.VMEM((whole + rows, LANES), jnp.float32),
+            pltpu.SemaphoreType.DMA((32,)),
+        ],
+        compiler_params=pltpu.CompilerParams(vmem_limit_bytes=VMEM_CAP),
+    )(jnp.reshape(me, (1,)), *mats, vec_rows)
+
+
+def gather_weights(values, device, cols, vec_cols):
+    shard = values.shape[0]
+    count = lax.axis_size("sent")
+    if is_grid(count, shard):
+        pieces = gather_pieces(pack_shard(values, device))
+        mats, vec_rows = unflatten(pieces, device, shard, cols)
+        return mats, vec_rows.reshape(D, vec_cols)
+    full = lax.all_gather(values.astype(jnp.bfloat16), "sent", axis=0, tiled=True)
+    split = D * cols * LANES
+    vecs = full[split:].reshape(D, vec_cols).astype(jnp.float32)
+    return full[:split].reshape(D, cols * LANES), vecs
+
+
+def scatter_grads(mats, vecs, device, shard):
+    count = lax.axis_size("sent")
+    if is_grid(count, shard):
+        pieces = flatten([m.astype(jnp.bfloat16) for m in mats], vecs.reshape(-1, LANES), device, shard)
+        return unpack_shard(scatter_pieces(list(pieces)), device, shard)
+    flat = jnp.concatenate([jnp.concatenate(mats, axis=1).reshape(-1), vecs.reshape(-1)])
+    return lax.psum_scatter(flat, "sent", scatter_dimension=0, tiled=True)
+
+
+def gather_small(value, device):
+    count = lax.axis_size("sent")
+    if count != 32:
+        return lax.all_gather(value, "sent", axis=0)
+    got = jnp.stack([value, swap(value, CORE)])
+    got = jnp.concatenate([got] + [swap(got, bit) for bit in (XBIT, YBIT, XBIT | YBIT)])
+    got = jnp.concatenate([got] + [swap(got, bit) for bit in ZBITS])
+    return jnp.take(got, jnp.arange(count) ^ device, axis=0)
+
+
+def sum_small(value):
+    if lax.axis_size("sent") != 32:
+        return lax.psum(value, "sent")
+    value = value + swap(value, CORE)
+    across = [swap(value, bit) for bit in (XBIT, YBIT, XBIT | YBIT)]
+    value = (value + across[0]) + (across[1] + across[2])
+    along = [swap(value, bit) for bit in ZBITS]
+    return (value + along[0]) + (along[1] + along[2])
 
 
 def on_device(
@@ -91,15 +341,9 @@
     slot_count = lengths.shape[0]
     all_rows = 2 * tok_rows
     device = lax.axis_index("sent")
-    attn_full, head_full = (
-        lax.all_gather(attn_params.astype(jnp.bfloat16), "sent", axis=0, tiled=True),
-        lax.all_gather(head_params.astype(jnp.bfloat16), "sent", axis=0, tiled=True),
-    )
-    attn_mats = attn_full[: 4 * D * D].reshape(D, 4 * D)
-    attn_vecs_low = attn_full[4 * D * D :].reshape(D, 8 + POS)
-    attn_vecs = attn_vecs_low.astype(jnp.float32)
-    head_mats = head_full[: 9 * D * D].reshape(D, 9 * D)
-    head_vecs = head_full[9 * D * D :].reshape(D, 8).astype(jnp.float32)
+    attn_mats, attn_vecs = gather_weights(attn_params, device, 24, 8 + POS)
+    head_mats, head_vecs = gather_weights(head_params, device, 54, 8)
+    attn_vecs_low = attn_vecs.astype(jnp.bfloat16)
     w_qkv = attn_mats[:, : 3 * D]
     w_out = attn_mats[:, 3 * D :]
     w_up = head_mats[:, : 4 * D]
@@ -179,37 +423,33 @@
     pooled = jnp.tanh(plain_dot(cls_low, w_pool) + head_vecs[:, 7])
     unit_rows, unit_back = jax.vjp(unit_scale, pooled)
     unit_low = unit_rows.astype(jnp.bfloat16)
-    query_embeddings = unit_low[:slot_count]
-    positive_view_set = unit_low[slot_count:]
-    target_sentence_set, everyone = (
-        lax.all_gather(positive_view_set, "sent", axis=0, tiled=True),
-        lax.all_gather(query_embeddings, "sent", axis=0, tiled=True),
-    )
-    own_cols = device * slot_count + slot_ids
-    col_ids = jnp.arange(target_sentence_set.shape[0], dtype=jnp.int32)
-    pos_hot = col_ids[None, :] == own_cols[:, None]
+    units = gather_small(unit_low, device)
+    anchors = units[:, :slot_count].reshape(-1, D)
+    partners = units[:, slot_count:].reshape(-1, D)
+    slots_all = anchors.shape[0]
     cosine_logit_table = jnp.where(
         valid_everything[None, :] > 0,
-        target_dot_terms(query_embeddings, target_sentence_set) / logit_divisor,
+        target_dot_terms(anchors, partners) / logit_divisor,
         masked_scores,
     )
+    diagonal = jnp.arange(slots_all)[:, None] == jnp.arange(slots_all)[None, :]
     sim_top = jnp.max(cosine_logit_table, axis=-1, keepdims=True)
-    row_lse = sim_top[:, 0] + jnp.log(jnp.sum(jnp.exp(cosine_logit_table - sim_top), axis=-1))
-    positive = jnp.sum(jnp.where(pos_hot, cosine_logit_table, 0.0), axis=-1)
-    local_loss = jnp.sum(valid_own * (row_lse - positive))
-    loss_sum = lax.psum(local_loss, "sent")
-    cosine_logit_cotangent = valid_own[:, None] * (
-        jnp.exp(cosine_logit_table - row_lse[:, None]) - pos_hot.astype(jnp.float32)
-    )
-    cosine_logit_summed = (cosine_logit_cotangent / logit_divisor).astype(jnp.bfloat16)
-    d_anchor = plain_dot(cosine_logit_summed, target_sentence_set)
-    all_lse = lax.all_gather(row_lse, "sent", axis=0, tiled=True)
-    back_sim = target_dot_terms(everyone, positive_view_set) / logit_divisor
-    back_hot = (col_ids[:, None] == own_cols[None, :]).astype(jnp.float32)
-    back_grad = valid_everything[:, None] * (
-        jnp.exp(back_sim - all_lse[:, None]) * valid_own[None, :] - back_hot
-    )
-    d_partner = rows_dot((back_grad / logit_divisor).astype(jnp.bfloat16), everyone)
+    row_lse = sim_top + jnp.log(
+        jnp.sum(jnp.exp(cosine_logit_table - sim_top), axis=-1, keepdims=True)
+    )
+    positive = jnp.sum(jnp.where(diagonal, cosine_logit_table, 0.0), axis=-1)
+    loss_sum = jnp.sum(valid_everything * (row_lse[:, 0] - positive))
+    sim_low = (
+        valid_everything[:, None]
+        * (jnp.exp(cosine_logit_table - row_lse) - diagonal.astype(jnp.float32))
+        / logit_divisor
+    ).astype(jnp.bfloat16)
+    d_anchor = lax.dynamic_slice(
+        plain_dot(sim_low, partners), (device * slot_count, 0), (slot_count, D)
+    )
+    d_partner = lax.dynamic_slice(
+        rows_dot(sim_low, anchors), (device * slot_count, 0), (slot_count, D)
+    )
     d_unit = jnp.concatenate([d_anchor, d_partner], axis=0)
     d_pooled = unit_back(d_unit)[0]
     d_pool_pre = d_pooled * (1.0 - pooled * pooled)
@@ -241,9 +481,7 @@
         ],
         axis=1,
     )
-    head_grad = jnp.concatenate(
-        [jnp.concatenate([g_up, g_down, g_pool], axis=1).reshape(-1), head_vec_grad.reshape(-1)]
-    )
+    head_share = scatter_grads([g_up, g_down, g_pool], head_vec_grad, device, head_params.shape[0])
     d_first_res, g_gain_one, g_shift_one = first_back(d_first)
     d_branch = d_first_res * keep_attn
     g_out_bias = jnp.sum(d_branch, axis=0)
@@ -305,15 +543,9 @@
         ],
         axis=1,
     )
-    attn_grad = jnp.concatenate(
-        [jnp.concatenate([g_qkv, g_out], axis=1).reshape(-1), attn_vec_grad.reshape(-1)]
-    )
-    attn_share, head_share = (
-        lax.psum_scatter(attn_grad, "sent", scatter_dimension=0, tiled=True),
-        lax.psum_scatter(head_grad, "sent", scatter_dimension=0, tiled=True),
-    )
+    attn_share = scatter_grads([g_qkv, g_out], attn_vec_grad, device, attn_params.shape[0])
     squares = jnp.sum(attn_share * attn_share) + jnp.sum(head_share * head_share)
-    total_squares = lax.psum(squares, "sent")
+    total_squares = sum_small(squares)
     loss = loss_sum / jnp.sum(valid_everything)
     grad_norm = jnp.sqrt(total_squares)
     clip_scale = jnp.minimum(1.0, clip_bound / grad_norm)

time: 1210 us -> 469 us (0.39)
  waiting for transfers between devices: 722 us -> 148 us
  blocking collectives: 156 us -> 0 us
  starting transfers between devices: 0.08 us -> 93.3 us
  local copies, waits for them, and re-layouts: 127 us -> 47.4 us
  other arithmetic: 82 us -> 35.8 us
  Pallas kernels: 0 us -> 37 us
    unnamed x4 -> x0, waiting for transfers between devices: 722 us -> none
    ppermute x0 -> x78, waiting for transfers between devices: none -> 148 us  [swap(): return lax.ppermute(value, 'sent', [(i, i ^ bit) for i in range(count)])]
    ppermute x0 -> x78, starting transfers between devices: none -> 93.3 us  [swap(): return lax.ppermute(value, 'sent', [(i, i ^ bit) for i in range(count)])]
    all_gather x2 -> x0, blocking collectives: 78.7 us -> none  [the longest x1 41 us: on_device(): lax.all_gather(query_embeddings, 'sent', axis=0, tiled=True)]
    psum x1 -> x0, blocking collectives: 39.9 us -> none  [on_device(): loss_sum = lax.psum(local_loss, 'sent')]
    reshape x5 -> x4, local copies, waits for them, and re-layouts: 44.8 us -> 5.36 us  [the longest x2 3 us: gather_weights(): return (mats, vec_rows.reshape(D, vec_cols))]
    concatenate x3 -> x2, other arithmetic: 41.4 us -> 3.47 us  [gather_pieces(): jnp.concatenate([low_half, high_half])]
    unnamed x1 -> x0, blocking collectives: 37.4 us -> none
  transfers between devices with their start and end apart: 2 -> 78, of which waited for: 2 -> 31; matrix products, arithmetic and copies ran while one was open for 1% -> 12% of each run, Pallas kernels for 0% -> 4%
where the time goes in v1:
time: 469 us; the launch traced here: 464 us
  waiting for transfers between devices  148 us (32%)
  starting transfers between devices  93.3 us (20%)
  matrix products  87.3 us (19%)
  local copies, waits for them, and re-layouts  47.4 us (10%)
  Pallas kernels  37 us (8%)
  other arithmetic  35.8 us (8%)
  between operations  15.2 us (3%)
    ppermute x78, waiting for transfers between devices, swap(): return lax.ppermute(value, 'sent', [(i, i ^ bit) for i in range(count)])  148 us
    ppermute x78, starting transfers between devices, swap(): return lax.ppermute(value, 'sent', [(i, i ^ bit) for i in range(count)])  93.3 us
    dot_general x6, matrix products, rows_dot(): lax.dot_general(left_op, right_op, (((0,), (0,)), ((), ())), preferred_el...  22.1 us
    dot_general x7, matrix products, plain_dot(): return jnp.dot(left_op, right_op, preferred_element_type=jnp.float32)  21.9 us
    pallas_call x2, Pallas kernels, unflatten(): pl.pallas_call(functools.partial(unflatten_kernel, shard, cols), out_shap...  20.1 us
    dot_general x6, matrix products, target_dot_terms(): lax.dot_general(left_op, right_op, (((1,), (1,)), ((), ())), preferred_el...  19.9 us
    pallas_call x2, Pallas kernels, flatten(): pl.pallas_call(functools.partial(flatten_kernel, shard, widths), out_shap...  16.9 us
    unnamed x182, local copies, waits for them, and re-layouts  15.9 us
  transfers between devices with their start and end apart: 78, of which 31 were waited for; matrix products, arithmetic and copies ran while one was open for 12% of the time, Pallas kernels for 4%

profile of v1, /device:TPU:0, one launch (start us, length us, event | category | flops | bytes accessed | tf_op | source)
XLA Modules:
  0.0 463.6 jit_solution(3891868655520583361)
XLA Ops:
  3.1 5.0 %collective-permute-start.18 = (bf16[1312,128]{1,0:T(8,128)(2,1)}, bf16[1312,128]{1,0:T(8,128)(2,1)S(1)}, u32[]{:S(2)}, u32[]{:S(2)}) collective-permute-start(bf16[1312,128]{1,0:T(8,128)(2,1)} %fusion.79), channel_id=1, source_target_pairs={{0,24},{1,25},{2,26},{3,27},{4,28},{5,29},{6,30},{7,31},{8,16},{9,... | collective-permute-start | bytes 1007624 | tf_op jit(solution)/shard_map/ppermute | solution.py:86
  8.9 1.9 collective-permute-start.2
  19.0 2.8 convert_multiply_fusion
  21.8 2.2 copy-done
  24.0 2.1 fusion.133
  28.0 5.1 %collective-permute-done = bf16[624,128]{1,0:T(8,128)(2,1)} collective-permute-done((bf16[624,128]{1,0:T(8,128)(2,1)}, bf16[624,128]{1,0:T(8,128)(2,1)}, u32[]{:S(2)}, u32[]{:S(2)}) %collective-permute-start) | collective-permute-done | bytes 159776 | tf_op jit(solution)/shard_map/ppermute | solution.py:86
  37.7 11.0 %collective-permute-start.16 = (bf16[1312,128]{1,0:T(8,128)(2,1)}, bf16[1312,128]{1,0:T(8,128)(2,1)S(1)}, u32[]{:S(2)}, u32[]{:S(2)}) collective-permute-start(bf16[1312,128]{1,0:T(8,128)(2,1)} %fusion.79), channel_id=1, source_target_pairs={{0,8},{1,9},{2,10},{3,11},{4,12},{5,13},{6,14},{7,15},{8,0},{9,1},... | collective-permute-start | bytes 1007624 | tf_op jit(solution)/shard_map/ppermute | solution.py:86
  48.7 2.0 collective-permute-done.1
  57.7 10.5 %collective-permute-done.4.refs_2_ = bf16[2,624,128]{2,1,0:T(8,128)(2,1)S(1)} collective-permute-done((bf16[2,624,128]{2,1,0:T(8,128)(2,1)S(1)}, bf16[2,624,128]{2,1,0:T(8,128)(2,1)S(1)}, u32[]{:S(2)}, u32[]{:S(2)}) %collective-permute-start.4) | collective-permute-done | bytes 319520 | tf_op jit(solution)/shard_map/ppermute | solution.py:86
  70.3 3.0 collective-permute-done.7.refs_5_
  81.6 2.3 pad_maximum_fusion.refs_0_
  83.9 9.7 %collective-permute-done.19.refs_1_ = bf16[2,1312,128]{2,1,0:T(8,128)(2,1)} collective-permute-done((bf16[2,1312,128]{2,1,0:T(8,128)(2,1)}, bf16[2,1312,128]{2,1,0:T(8,128)(2,1)}, u32[]{:S(2)}, u32[]{:S(2)}) %collective-permute-start.19) | collective-permute-done | bytes 671776 | tf_op jit(solution)/shard_map/ppermute | solution.py:86
  95.1 12.2 %collective-permute-done.20.refs_2_ = bf16[2,1312,128]{2,1,0:T(8,128)(2,1)} collective-permute-done((bf16[2,1312,128]{2,1,0:T(8,128)(2,1)}, bf16[2,1312,128]{2,1,0:T(8,128)(2,1)}, u32[]{:S(2)}, u32[]{:S(2)}) %collective-permute-start.20) | collective-permute-done | bytes 671776 | tf_op jit(solution)/shard_map/ppermute | solution.py:86
  110.6 8.0 %shard_map.220 = (bf16[768,3072]{1,0:T(8,128)(2,1)}, f32[816,128]{1,0:T(8,128)}) custom-call(s32[1]{0:T(128)} %bitcast.1.me_ref, bf16[4,624,128]{2,1,0:T(8,128)(2,1)} %copy-done.24, bf16[2,624,128]{2,1,0:T(8,128)(2,1)} %copy-done.63, bf16[2,624,128]{2,1,0:T(8,128)(2,1)} %copy-done.64, bf16[2,624,128]{2,1,0:T(8,128)(2,1)} %collective-permute-done.5.refs_3_, ...), custom_call_target="tpu_custom_call" | custom-call | tf_op jit(solution)/shard_map/pallas_call | solution.py:212
  118.5 2.0 reshape.440
  126.3 2.0 fusion.1
  128.3 2.5 copy.70
  130.8 4.2 reshape.441
  142.4 2.3 fusion.138
  147.9 12.1 %shard_map.221 = (bf16[768,6912]{1,0:T(8,128)(2,1)}, f32[48,128]{1,0:T(8,128)}) custom-call(s32[1]{0:T(128)} %bitcast.1.me_ref, bf16[4,1312,128]{2,1,0:T(8,128)(2,1)} %pad_maximum_fusion.refs_0_, bf16[2,1312,128]{2,1,0:T(8,128)(2,1)} %collective-permute-done.19.refs_1_, bf16[2,1312,128]{2,1,0:T(8,128)(2,1)} %collective-permute-done.20.refs_2_, ...), custom_call_target="tpu_custom_call" | custom-call | tf_op jit(solution)/shard_map/pallas_call | solution.py:212
  162.2 6.7 %multiply_convert_fusion = (bf16[512,3072]{1,0:T(8,128)(2,1)S(1)}, f32[512,3072]{1,0:T(8,128)}) fusion(f32[3072]{0:T(1024)S(1)} %add.501, bf16[768,6912]{1,0:T(8,128)(2,1)} %get-tuple-element.46, f32[512,768]{1,0:T(8,128)S(1)} %get-tuple-element.168, f32[768]{0:T(1024)S(1)} %get-tuple-element.84, f32[768]{0:T(1024)S(1)} %get-tuple-element.83, ...), kind=kOutput, calls=%fused_computation.4 | convolution fusion | flops 2427322368 | bytes 15751168 | tf_op jit(solution)/shard_map/dot_general | solution.py:53
  168.9 6.9 %fusion.139 = (f32[512]{0:T(512)S(1)}, f32[512,768]{1,0:T(8,128)S(1)}) fusion(f32[768]{0:T(1024)S(1)} %get-tuple-element.94, bf16[512,3072]{1,0:T(8,128)(2,1)S(1)} %get-tuple-element.169, bf16[768,6912]{1,0:T(8,128)(2,1)} %get-tuple-element.46, f32[2,1,256,768]{3,2,1,0:T(8,128)S(1)} %copy-done.11, f32[768]{0:T(1024)S(1)} %get-tuple-element.84, ...), kind=kOutput, calls=%fused_computation.300 | convolution fusion | flops 2419064320 | bytes 12598272 | tf_op jit(solution)/shard_map/dot_general | solution.py:63
  183.5 1.8 collective-permute-start.35
  189.1 3.2 collective-permute-start.37
  193.6 4.0 collective-permute-done.36
  198.2 8.1 %collective-permute-done.37 = bf16[8,16,768]{2,1,0:T(8,128)(2,1)S(1)} collective-permute-done((bf16[8,16,768]{2,1,0:T(8,128)(2,1)S(1)}, bf16[8,16,768]{2,1,0:T(8,128)(2,1)S(1)}, u32[]{:S(2)}, u32[]{:S(2)}) %collective-permute-start.37) | collective-permute-done | bytes 196640 | tf_op jit(solution)/shard_map/ppermute | solution.py:86
  216.7 8.4 %fusion.143 = (f32[3072]{0:T(1024)S(1)}, bf16[512,3072]{1,0:T(8,128)(2,1)S(1)}) fusion(bf16[768,6912]{1,0:T(8,128)(2,1)} %get-tuple-element.46, bf16[512,768]{1,0:T(8,128)(2,1)S(1)} %get-tuple-element.110, f32[512,3072]{1,0:T(8,128)} %get-tuple-element.170, f32[3072]{0:T(1024)S(1)} %add.501), kind=kOutput, calls=%fused_computation.302 | convolution fusion | flops 2439508992 | bytes 14966784 | tf_op jit(solution)/shard_map/dot_general | solution.py:53
  225.1 6.7 %multiply_reduce_fusion.1 = (f32[768]{0:T(1024)S(1)}, f32[512]{0:T(512)S(1)}, f32[768]{0:T(1024)S(1)}, f32[512,768]{1,0:T(8,128)S(1)}) fusion(f32[512,768]{1,0:T(8,128)S(1)} %copy-done.4, f32[512]{0:T(512)S(1)} %fusion.107, f32[512]{0:T(512)S(1)} %broadcast_multiply_fusion.1, f32[768]{0:T(1024)S(1)} %get-tuple-element.83, ...), kind=kOutput, calls=%fused_computation.61 | convolution fusion | flops 2419849216 | bytes 12600320 | tf_op jit(solution)/shard_map/dot_general | solution.py:63
  234.6 2.1 convolution_convert_fusion.5
  239.6 3.6 fusion.74
  243.2 2.1 bitcast_reduce_fusion
  245.4 7.2 %fusion.48 = bf16[4,128,1,12,64]{1,4,3,0,2:T(8,128)(2,1)} fusion(f32[4,12,128,128]{2,3,1,0:T(8,128)} %fusion.74, f32[4,12,128,128]{2,3,1,0:T(8,128)} %copy-done.5, f32[4,12,128]{2,1,0:T(8,128)S(1)} %log_add_fusion, bf16[4,128,1,12,64]{1,0,4,3,2:T(4,128)(2,1)} %copy-done.33), kind=kOutput, calls=%fused_computation.78 | convolution fusion | flops 106174592 | bytes 7888896 | tf_op jit(solution)/shard_map/bhqk,bqhd->bkhd/dot_general | solution.py:510
  252.5 7.3 %bitcast_reduce_fusion.1 = (f32[12,64]{1,0:T(8,128)S(1)}, bf16[4,12,64,128]{3,2,1,0:T(8,128)(2,1)}) fusion(f32[4,12,128,128]{2,3,1,0:T(8,128)} %fusion.74, f32[4,12,128,128]{2,3,1,0:T(8,128)} %copy-done.5, f32[4,12,128]{2,1,0:T(8,128)S(1)} %log_add_fusion, bf16[4,128,1,12,64]{1,0,4,3,2:T(4,128)(2,1)} %copy-done.32), kind=kOutput, calls=%fused_computation.47 | convolution fusion | flops 106960256 | bytes 7891968 | tf_op jit(solution)/shard_map/bhqk,bkhd->bqhd/dot_general | solution.py:507
  259.8 3.1 convolution_convert_fusion.3.refs_1_
  263.0 6.7 %convolution_convert_fusion.1.refs_0_ = bf16[768,3072]{1,0:T(8,128)(2,1)} fusion(bf16[512,3072]{1,0:T(8,128)(2,1)} %copy-done.85, f32[512,768]{1,0:T(8,128)S(1)} %copy-done.4, f32[768]{0:T(1024)S(1)} %get-tuple-element.84, f32[768]{0:T(1024)S(1)} %get-tuple-element.83, f32[512]{0:T(512)S(1)} %fusion.107, f32[512]{0:T(512)S(1)} %broadcast_multiply_fusion.1), kind=kOutput, calls=%fused_computation.7 | convolution fusion | flops 2420244480 | bytes 9447424 | tf_op jit(solution)/shard_map/dot_general | solution.py:57
  270.0 2.3 copy.85
  272.4 2.3 fusion.37
  274.7 1.8 fusion.33
  277.2 3.9 convolution_convert_fusion.2.refs_0_
  284.0 6.8 %shard_map.222 = (bf16[4,624,128]{2,1,0:T(8,128)(2,1)}, bf16[2,624,128]{2,1,0:T(8,128)(2,1)}, bf16[2,624,128]{2,1,0:T(8,128)(2,1)}, bf16[2,624,128]{2,1,0:T(8,12...) custom-call(s32[1]{0:T(128)} %bitcast.1.me_ref, ...), custom_call_target="tpu_custom_call" | custom-call | tf_op jit(solution)/shard_map/pallas_call | solution.py:268
  290.9 6.5 %convolution_convert_fusion.refs_1_ = bf16[768,3072]{1,0:T(8,128)(2,1)} fusion(bf16[512,3072]{1,0:T(8,128)(2,1)} %copy-done.84, bf16[512,768]{1,0:T(8,128)(2,1)S(1)} %copy-done.38), kind=kOutput, calls=%fused_computation.6 | convolution fusion | flops 2418278400 | bytes 8650752 | tf_op jit(solution)/shard_map/dot_general | solution.py:57
  302.5 10.1 %shard_map.223 = (bf16[4,1312,128]{2,1,0:T(8,128)(2,1)}, bf16[2,1312,128]{2,1,0:T(8,128)(2,1)}, bf16[2,1312,128]{2,1,0:T(8,128)(2,1)}, bf16[2,1312,128]{2,1,0:T(...) custom-call(s32[1]{0:T(128)} %bitcast.1.me_ref, ...), custom_call_target="tpu_custom_call" | custom-call | tf_op jit(solution)/shard_map/pallas_call | solution.py:268
  316.4 7.1 %collective-permute-done.44 = bf16[2,624,128]{2,1,0:T(8,128)(2,1)S(1)} collective-permute-done((bf16[2,624,128]{2,1,0:T(8,128)(2,1)S(1)}, bf16[2,624,128]{2,1,0:T(8,128)(2,1)S(1)}, u32[]{:S(2)}, u32[]{:S(2)}) %collective-permute-start.44) | collective-permute-done | bytes 319520 | tf_op jit(solution)/shard_map/ppermute | solution.py:86
  331.4 14.2 %collective-permute-done.60 = bf16[2,1312,128]{2,1,0:T(8,128)(2,1)S(1)} collective-permute-done((bf16[2,1312,128]{2,1,0:T(8,128)(2,1)S(1)}, bf16[2,1312,128]{2,1,0:T(8,128)(2,1)S(1)}, u32[]{:S(2)}, u32[]{:S(2)}) %collective-permute-start.60) | collective-permute-done | bytes 671776 | tf_op jit(solution)/shard_map/ppermute | solution.py:86
  347.2 7.2 %collective-permute-done.41 = bf16[2,624,128]{2,1,0:T(8,128)(2,1)S(1)} collective-permute-done((bf16[2,624,128]{2,1,0:T(8,128)(2,1)S(1)}, bf16[2,624,128]{2,1,0:T(8,128)(2,1)S(1)}, u32[]{:S(2)}, u32[]{:S(2)}) %collective-permute-start.41) | collective-permute-done | bytes 319520 | tf_op jit(solution)/shard_map/ppermute | solution.py:86
  358.8 6.1 %collective-permute-done.52 = bf16[2,624,128]{2,1,0:T(8,128)(2,1)S(1)} collective-permute-done((bf16[2,624,128]{2,1,0:T(8,128)(2,1)S(1)}, bf16[2,624,128]{2,1,0:T(8,128)(2,1)S(1)}, u32[]{:S(2)}, u32[]{:S(2)}) %collective-permute-start.52) | collective-permute-done | bytes 319520 | tf_op jit(solution)/shard_map/ppermute | solution.py:86
  366.0 5.7 %collective-permute-done.45 = bf16[2,624,128]{2,1,0:T(8,128)(2,1)S(1)} collective-permute-done((bf16[2,624,128]{2,1,0:T(8,128)(2,1)S(1)}, bf16[2,624,128]{2,1,0:T(8,128)(2,1)S(1)}, u32[]{:S(2)}, u32[]{:S(2)}) %collective-permute-start.45) | collective-permute-done | bytes 319520 | tf_op jit(solution)/shard_map/ppermute | solution.py:86
  374.5 2.1 collective-permute-start.54
  376.6 4.7 %collective-permute-done.57 = bf16[2,1312,128]{2,1,0:T(8,128)(2,1)S(1)} collective-permute-done((bf16[2,1312,128]{2,1,0:T(8,128)(2,1)S(1)}, bf16[2,1312,128]{2,1,0:T(8,128)(2,1)S(1)}, u32[]{:S(2)}, u32[]{:S(2)}) %collective-permute-start.57) | collective-permute-done | bytes 671776 | tf_op jit(solution)/shard_map/ppermute | solution.py:86
  381.3 2.9 collective-permute-start.53
  384.2 1.9 collective-permute-done.68
  386.1 2.0 collective-permute-start.46
  388.1 9.8 %collective-permute-done.61 = bf16[2,1312,128]{2,1,0:T(8,128)(2,1)S(1)} collective-permute-done((bf16[2,1312,128]{2,1,0:T(8,128)(2,1)S(1)}, bf16[2,1312,128]{2,1,0:T(8,128)(2,1)S(1)}, u32[]{:S(2)}, u32[]{:S(2)}) %collective-permute-start.61) | collective-permute-done | bytes 671776 | tf_op jit(solution)/shard_map/ppermute | solution.py:86
  398.6 2.1 collective-permute-start.70
  404.1 7.3 %collective-permute-done.70 = bf16[1312,128]{1,0:T(8,128)(2,1)S(1)} collective-permute-done((bf16[1312,128]{1,0:T(8,128)(2,1)S(1)}, bf16[1312,128]{1,0:T(8,128)(2,1)S(1)}, u32[]{:S(2)}, u32[]{:S(2)}) %collective-permute-start.70) | collective-permute-done | bytes 335904 | tf_op jit(solution)/shard_map/ppermute | solution.py:86
  411.4 17.5 %collective-permute-done.69 = bf16[1312,128]{1,0:T(8,128)(2,1)S(1)} collective-permute-done((bf16[1312,128]{1,0:T(8,128)(2,1)S(1)}, bf16[1312,128]{1,0:T(8,128)(2,1)S(1)}, u32[]{:S(2)}, u32[]{:S(2)}) %collective-permute-start.69) | collective-permute-done | bytes 335904 | tf_op jit(solution)/shard_map/ppermute | solution.py:86
  433.5 2.7 collective-permute-start.72
  436.2 2.4 collective-permute-start.73
  438.6 2.4 collective-permute-start.74
  445.7 4.2 collective-permute-start.76
  449.9 2.8 collective-permute-start.77
  453.3 2.0 collective-permute-done.77
  456.7 2.5 multiply_add_fusion.7
  459.1 2.0 multiply_add_fusion.5
  (446 shorter events, 122.4 us)
Async XLA Ops:
  3.1 49.2 %collective-permute-start.18 = (bf16[1312,128]{1,0:T(8,128)(2,1)}, bf16[1312,128]{1,0:T(8,128)(2,1)S(1)}, u32[]{:S(2)}, u32[]{:S(2)}) collective-permute-start(bf16[1312,128]{1,0:T(8,128)(2,1)} %fusion.79), channel_id=1, source_target_pairs={{0,24},{1,25},{2,26},{3,27},{4,28},{5,29},{6,30},{7,31},{8,16},{9,... | collective-permute-start | bytes 1007624 | tf_op jit(solution)/shard_map/ppermute | solution.py:86
  8.1 44.8 %collective-permute-start.17 = (bf16[1312,128]{1,0:T(8,128)(2,1)}, bf16[1312,128]{1,0:T(8,128)(2,1)S(1)}, u32[]{:S(2)}, u32[]{:S(2)}) collective-permute-start(bf16[1312,128]{1,0:T(8,128)(2,1)} %fusion.79), channel_id=1, source_target_pairs={{0,16},{1,17},{2,18},{3,19},{4,20},{5,21},{6,22},{7,23},{8,24},{9,... | collective-permute-start | bytes 1007624 | tf_op jit(solution)/shard_map/ppermute | solution.py:86
  8.9 28.8 %collective-permute-start.2 = (bf16[624,128]{1,0:T(8,128)(2,1)}, bf16[624,128]{1,0:T(8,128)(2,1)S(1)}, u32[]{:S(2)}, u32[]{:S(2)}) collective-permute-start(bf16[624,128]{1,0:T(8,128)(2,1)} %fusion.90), channel_id=1, source_target_pairs={{0,24},{1,25},{2,26},{3,27},{4,28},{5,29},{6,30},{7,31},{8,16},{9,... | collective-permute-start | bytes 479240 | tf_op jit(solution)/shard_map/ppermute | solution.py:86
  10.9 39.9 %collective-permute-start.1 = (bf16[624,128]{1,0:T(8,128)(2,1)}, bf16[624,128]{1,0:T(8,128)(2,1)S(1)}, u32[]{:S(2)}, u32[]{:S(2)}) collective-permute-start(bf16[624,128]{1,0:T(8,128)(2,1)} %fusion.90), channel_id=1, source_target_pairs={{0,16},{1,17},{2,18},{3,19},{4,20},{5,21},{6,22},{7,23},{8,24},{9,... | collective-permute-start | bytes 479240 | tf_op jit(solution)/shard_map/ppermute | solution.py:86
  11.9 21.2 %collective-permute-start = (bf16[624,128]{1,0:T(8,128)(2,1)}, bf16[624,128]{1,0:T(8,128)(2,1)}, u32[]{:S(2)}, u32[]{:S(2)}) collective-permute-start(bf16[624,128]{1,0:T(8,128)(2,1)} %fusion.90), channel_id=1, source_target_pairs={{0,8},{1,9},{2,10},{3,11},{4,12},{5,13},{6,14},{7,15},{8,0},{9,1},... | collective-permute-start | bytes 479240 | tf_op jit(solution)/shard_map/ppermute | solution.py:86
  34.8 19.6 %collective-permute-start.5 = (bf16[2,624,128]{2,1,0:T(8,128)(2,1)}, bf16[2,624,128]{2,1,0:T(8,128)(2,1)}, u32[]{:S(2)}, u32[]{:S(2)}) collective-permute-start(bf16[2,624,128]{2,1,0:T(8,128)(2,1)} %pad_maximum_fusion.4), channel_id=1, source_target_pairs={{0,4},{1,5},{2,6},{3,7},{4,0},{5,1},{6,2},{7,3},{8,12},{9,13},{10,... | collective-permute-start | bytes 958472 | tf_op jit(solution)/shard_map/ppermute | solution.py:86
  37.7 20.0 %collective-permute-start.16 = (bf16[1312,128]{1,0:T(8,128)(2,1)}, bf16[1312,128]{1,0:T(8,128)(2,1)S(1)}, u32[]{:S(2)}, u32[]{:S(2)}) collective-permute-start(bf16[1312,128]{1,0:T(8,128)(2,1)} %fusion.79), channel_id=1, source_target_pairs={{0,8},{1,9},{2,10},{3,11},{4,12},{5,13},{6,14},{7,15},{8,0},{9,1},... | collective-permute-start | bytes 1007624 | tf_op jit(solution)/shard_map/ppermute | solution.py:86
  50.7 19.1 %collective-permute-start.3 = (bf16[2,624,128]{2,1,0:T(8,128)(2,1)}, bf16[2,624,128]{2,1,0:T(8,128)(2,1)S(1)}, u32[]{:S(2)}, u32[]{:S(2)}) collective-permute-start(bf16[2,624,128]{2,1,0:T(8,128)(2,1)} %pad_maximum_fusion.4), channel_id=1, source_target_pairs={{0,2},{1,3},{2,0},{3,1},{4,6},{5,7},{6,4},{7,5},{8,10},{9,11},{10,... | collective-permute-start | bytes 958472 | tf_op jit(solution)/shard_map/ppermute | solution.py:86
  52.3 16.0 %collective-permute-start.4 = (bf16[2,624,128]{2,1,0:T(8,128)(2,1)S(1)}, bf16[2,624,128]{2,1,0:T(8,128)(2,1)S(1)}, u32[]{:S(2)}, u32[]{:S(2)}) collective-permute-start(bf16[2,624,128]{2,1,0:T(8,128)(2,1)S(1)} %pad_maximum_fusion.5), channel_id=1, source_target_pairs={{0,2},{1,3},{2,0},{3,1},{4,6},{5,7},{6,4},{7,5},{8,10},{9,11},{10,... | collective-permute-start | bytes 958472 | tf_op jit(solution)/shard_map/ppermute | solution.py:86
  52.9 16.9 %collective-permute-start.6 = (bf16[2,624,128]{2,1,0:T(8,128)(2,1)S(1)}, bf16[2,624,128]{2,1,0:T(8,128)(2,1)S(1)}, u32[]{:S(2)}, u32[]{:S(2)}) collective-permute-start(bf16[2,624,128]{2,1,0:T(8,128)(2,1)S(1)} %pad_maximum_fusion.5), channel_id=1, source_target_pairs={{0,4},{1,5},{2,6},{3,7},{4,0},{5,1},{6,2},{7,3},{8,12},{9,13},{10,... | collective-permute-start | bytes 958472 | tf_op jit(solution)/shard_map/ppermute | solution.py:86
  54.4 18.9 %collective-permute-start.7 = (bf16[2,624,128]{2,1,0:T(8,128)(2,1)}, bf16[2,624,128]{2,1,0:T(8,128)(2,1)}, u32[]{:S(2)}, u32[]{:S(2)}) collective-permute-start(bf16[2,624,128]{2,1,0:T(8,128)(2,1)} %collective-permute-done.5.refs_3_), channel_id=1, source_target_pairs={{0,2},{1,3},{2,0},{3,1},{4,6},{5,7},{6,4},{7,5},{8,10},{9,11},{10,... | collective-permute-start | bytes 958472 | tf_op jit(solution)/shard_map/ppermute | solution.py:86
  57.7 22.9 %collective-permute-start.9 = (bf16[4,624,128]{2,1,0:T(8,128)(2,1)S(1)}, bf16[4,624,128]{2,1,0:T(8,128)(2,1)S(1)}, u32[]{:S(2)}, u32[]{:S(2)}) collective-permute-start(bf16[4,624,128]{2,1,0:T(8,128)(2,1)S(1)} %pad_maximum_fusion.3.refs_0_), channel_id=1, source_target_pairs={{0,1},{1,0},{2,3},{3,2},{4,5},{5,4},{6,7},{7,6},{8,9},{9,8},{10,11... | collective-permute-start | bytes 1916936 | tf_op jit(solution)/shard_map/ppermute | solution.py:86
  68.3 7.1 %collective-permute-start.8 = (bf16[2,624,128]{2,1,0:T(8,128)(2,1)S(1)}, bf16[2,624,128]{2,1,0:T(8,128)(2,1)}, u32[]{:S(2)}, u32[]{:S(2)}) collective-permute-start(bf16[2,624,128]{2,1,0:T(8,128)(2,1)S(1)} %collective-permute-done.4.refs_2_), channel_id=1, source_target_pairs={{0,4},{1,5},{2,6},{3,7},{4,0},{5,1},{6,2},{7,3},{8,12},{9,13},{10,... | collective-permute-start | bytes 958472 | tf_op jit(solution)/shard_map/ppermute | solution.py:86
  69.8 8.6 %collective-permute-start.11 = (bf16[2,624,128]{2,1,0:T(8,128)(2,1)S(1)}, bf16[2,624,128]{2,1,0:T(8,128)(2,1)S(1)}, u32[]{:S(2)}, u32[]{:S(2)}) collective-permute-start(bf16[2,624,128]{2,1,0:T(8,128)(2,1)S(1)} %collective-permute-done.4.refs_2_), channel_id=1, source_target_pairs={{0,1},{1,0},{2,3},{3,2},{4,5},{5,4},{6,7},{7,6},{8,9},{9,8},{10,11... | collective-permute-start | bytes 958472 | tf_op jit(solution)/shard_map/ppermute | solution.py:86
  69.8 9.1 %collective-permute-start.12 = (bf16[2,624,128]{2,1,0:T(8,128)(2,1)}, bf16[2,624,128]{2,1,0:T(8,128)(2,1)S(1)}, u32[]{:S(2)}, u32[]{:S(2)}) collective-permute-start(bf16[2,624,128]{2,1,0:T(8,128)(2,1)} %collective-permute-done.5.refs_3_), channel_id=1, source_target_pairs={{0,1},{1,0},{2,3},{3,2},{4,5},{5,4},{6,7},{7,6},{8,9},{9,8},{10,11... | collective-permute-start | bytes 958472 | tf_op jit(solution)/shard_map/ppermute | solution.py:86
  75.4 18.2 %collective-permute-start.19 = (bf16[2,1312,128]{2,1,0:T(8,128)(2,1)}, bf16[2,1312,128]{2,1,0:T(8,128)(2,1)}, u32[]{:S(2)}, u32[]{:S(2)}) collective-permute-start(bf16[2,1312,128]{2,1,0:T(8,128)(2,1)} %pad_maximum_fusion.1), channel_id=1, source_target_pairs={{0,2},{1,3},{2,0},{3,1},{4,6},{5,7},{6,4},{7,5},{8,10},{9,11},{10,... | collective-permute-start | bytes 2015240 | tf_op jit(solution)/shard_map/ppermute | solution.py:86
  76.9 32.0 %collective-permute-start.21 = (bf16[2,1312,128]{2,1,0:T(8,128)(2,1)}, bf16[2,1312,128]{2,1,0:T(8,128)(2,1)}, u32[]{:S(2)}, u32[]{:S(2)}) collective-permute-start(bf16[2,1312,128]{2,1,0:T(8,128)(2,1)} %pad_maximum_fusion.1), channel_id=1, source_target_pairs={{0,4},{1,5},{2,6},{3,7},{4,0},{5,1},{6,2},{7,3},{8,12},{9,13},{10,... | collective-permute-start | bytes 2015240 | tf_op jit(solution)/shard_map/ppermute | solution.py:86
  78.4 28.9 %collective-permute-start.20 = (bf16[2,1312,128]{2,1,0:T(8,128)(2,1)}, bf16[2,1312,128]{2,1,0:T(8,128)(2,1)}, u32[]{:S(2)}, u32[]{:S(2)}) collective-permute-start(bf16[2,1312,128]{2,1,0:T(8,128)(2,1)} %pad_maximum_fusion.2), channel_id=1, source_target_pairs={{0,2},{1,3},{2,0},{3,1},{4,6},{5,7},{6,4},{7,5},{8,10},{9,11},{10,... | collective-permute-start | bytes 2015240 | tf_op jit(solution)/shard_map/ppermute | solution.py:86
  80.5 28.3 %collective-permute-start.14 = (bf16[2,624,128]{2,1,0:T(8,128)(2,1)}, bf16[2,624,128]{2,1,0:T(8,128)(2,1)}, u32[]{:S(2)}, u32[]{:S(2)}) collective-permute-start(bf16[2,624,128]{2,1,0:T(8,128)(2,1)} %collective-permute-done.7.refs_5_), channel_id=1, source_target_pairs={{0,1},{1,0},{2,3},{3,2},{4,5},{5,4},{6,7},{7,6},{8,9},{9,8},{10,11... | collective-permute-start | bytes 958472 | tf_op jit(solution)/shard_map/ppermute | solution.py:86
  80.7 29.7 %collective-permute-start.15 = (bf16[2,624,128]{2,1,0:T(8,128)(2,1)}, bf16[2,624,128]{2,1,0:T(8,128)(2,1)}, u32[]{:S(2)}, u32[]{:S(2)}) collective-permute-start(bf16[2,624,128]{2,1,0:T(8,128)(2,1)} %collective-permute-done.8.refs_6_), channel_id=1, source_target_pairs={{0,1},{1,0},{2,3},{3,2},{4,5},{5,4},{6,7},{7,6},{8,9},{9,8},{10,11... | collective-permute-start | bytes 958472 | tf_op jit(solution)/shard_map/ppermute | solution.py:86
  93.6 44.4 %collective-permute-start.22 = (bf16[2,1312,128]{2,1,0:T(8,128)(2,1)}, bf16[2,1312,128]{2,1,0:T(8,128)(2,1)}, u32[]{:S(2)}, u32[]{:S(2)}) collective-permute-start(bf16[2,1312,128]{2,1,0:T(8,128)(2,1)} %pad_maximum_fusion.2), channel_id=1, source_target_pairs={{0,4},{1,5},{2,6},{3,7},{4,0},{5,1},{6,2},{7,3},{8,12},{9,13},{10,... | collective-permute-start | bytes 2015240 | tf_op jit(solution)/shard_map/ppermute | solution.py:86
  107.3 34.1 %collective-permute-start.24 = (bf16[2,1312,128]{2,1,0:T(8,128)(2,1)}, bf16[2,1312,128]{2,1,0:T(8,128)(2,1)}, u32[]{:S(2)}, u32[]{:S(2)}) collective-permute-start(bf16[2,1312,128]{2,1,0:T(8,128)(2,1)} %collective-permute-done.20.refs_2_), channel_id=1, source_target_pairs={{0,4},{1,5},{2,6},{3,7},{4,0},{5,1},{6,2},{7,3},{8,12},{9,13},{10,... | collective-permute-start | bytes 2015240 | tf_op jit(solution)/shard_map/ppermute | solution.py:86
  108.8 33.1 %collective-permute-start.27 = (bf16[2,1312,128]{2,1,0:T(8,128)(2,1)}, bf16[2,1312,128]{2,1,0:T(8,128)(2,1)}, u32[]{:S(2)}, u32[]{:S(2)}) collective-permute-start(bf16[2,1312,128]{2,1,0:T(8,128)(2,1)} %collective-permute-done.20.refs_2_), channel_id=1, source_target_pairs={{0,1},{1,0},{2,3},{3,2},{4,5},{5,4},{6,7},{7,6},{8,9},{9,8},{10,11... | collective-permute-start | bytes 2015240 | tf_op jit(solution)/shard_map/ppermute | solution.py:86
  108.8 32.4 %collective-permute-start.23 = (bf16[2,1312,128]{2,1,0:T(8,128)(2,1)}, bf16[2,1312,128]{2,1,0:T(8,128)(2,1)}, u32[]{:S(2)}, u32[]{:S(2)}) collective-permute-start(bf16[2,1312,128]{2,1,0:T(8,128)(2,1)} %collective-permute-done.21.refs_3_), channel_id=1, source_target_pairs={{0,2},{1,3},{2,0},{3,1},{4,6},{5,7},{6,4},{7,5},{8,10},{9,11},{10,... | collective-permute-start | bytes 2015240 | tf_op jit(solution)/shard_map/ppermute | solution.py:86
  110.4 31.5 %collective-permute-start.26 = (bf16[2,1312,128]{2,1,0:T(8,128)(2,1)}, bf16[2,1312,128]{2,1,0:T(8,128)(2,1)}, u32[]{:S(2)}, u32[]{:S(2)}) collective-permute-start(bf16[2,1312,128]{2,1,0:T(8,128)(2,1)} %collective-permute-done.19.refs_1_), channel_id=1, source_target_pairs={{0,1},{1,0},{2,3},{3,2},{4,5},{5,4},{6,7},{7,6},{8,9},{9,8},{10,11... | collective-permute-start | bytes 2015240 | tf_op jit(solution)/shard_map/ppermute | solution.py:86
  139.5 6.2 %collective-permute-start.25 = (bf16[4,1312,128]{2,1,0:T(8,128)(2,1)S(1)}, bf16[4,1312,128]{2,1,0:T(8,128)(2,1)S(1)}, u32[]{:S(2)}, u32[]{:S(2)}) collective-permute-start(bf16[4,1312,128]{2,1,0:T(8,128)(2,1)S(1)} %copy-done.16), channel_id=1, source_target_pairs={{0,1},{1,0},{2,3},{3,2},{4,5},{5,4},{6,7},{7,6},{8,9},{9,8},{10,11... | collective-permute-start | bytes 4030472 | tf_op jit(solution)/shard_map/ppermute | solution.py:86
  142.0 6.0 %collective-permute-start.31 = (bf16[2,1312,128]{2,1,0:T(8,128)(2,1)}, bf16[2,1312,128]{2,1,0:T(8,128)(2,1)}, u32[]{:S(2)}, u32[]{:S(2)}) collective-permute-start(bf16[2,1312,128]{2,1,0:T(8,128)(2,1)} %collective-permute-done.24.refs_6_), channel_id=1, source_target_pairs={{0,1},{1,0},{2,3},{3,2},{4,5},{5,4},{6,7},{7,6},{8,9},{9,8},{10,11... | collective-permute-start | bytes 2015240 | tf_op jit(solution)/shard_map/ppermute | solution.py:86
  189.1 8.4 %collective-permute-start.36 = (bf16[8,16,768]{2,1,0:T(8,128)(2,1)S(1)}, bf16[8,16,768]{2,1,0:T(8,128)(2,1)S(1)}, u32[]{:S(2)}, u32[]{:S(2)}) collective-permute-start(bf16[8,16,768]{2,1,0:T(8,128)(2,1)S(1)} %get-tuple-element.153), channel_id=1, source_target_pairs={{0,8},{1,9},{2,10},{3,11},{4,12},{5,13},{6,14},{7,15},{8,0},{9,1},... | collective-permute-start | bytes 589832 | tf_op jit(solution)/shard_map/ppermute | solution.py:86
  189.1 17.2 %collective-permute-start.37 = (bf16[8,16,768]{2,1,0:T(8,128)(2,1)S(1)}, bf16[8,16,768]{2,1,0:T(8,128)(2,1)S(1)}, u32[]{:S(2)}, u32[]{:S(2)}) collective-permute-start(bf16[8,16,768]{2,1,0:T(8,128)(2,1)S(1)} %get-tuple-element.153), channel_id=1, source_target_pairs={{0,16},{1,17},{2,18},{3,19},{4,20},{5,21},{6,22},{7,23},{8,24},{9,... | collective-permute-start | bytes 589832 | tf_op jit(solution)/shard_map/ppermute | solution.py:86
  192.4 14.7 %collective-permute-start.38 = (bf16[8,16,768]{2,1,0:T(8,128)(2,1)S(1)}, bf16[8,16,768]{2,1,0:T(8,128)(2,1)S(1)}, u32[]{:S(2)}, u32[]{:S(2)}) collective-permute-start(bf16[8,16,768]{2,1,0:T(8,128)(2,1)S(1)} %get-tuple-element.153), channel_id=1, source_target_pairs={{0,24},{1,25},{2,26},{3,27},{4,28},{5,29},{6,30},{7,31},{8,16},{9,... | collective-permute-start | bytes 589832 | tf_op jit(solution)/shard_map/ppermute | solution.py:86
  290.8 21.8 %collective-permute-start.43 = (bf16[2,624,128]{2,1,0:T(8,128)(2,1)}, bf16[2,624,128]{2,1,0:T(8,128)(2,1)S(1)}, u32[]{:S(2)}, u32[]{:S(2)}) collective-permute-start(bf16[2,624,128]{2,1,0:T(8,128)(2,1)} %get-tuple-element.55), channel_id=1, source_target_pairs={{0,1},{1,0},{2,3},{3,2},{4,5},{5,4},{6,7},{7,6},{8,9},{9,8},{10,11... | collective-permute-start | bytes 958472 | tf_op jit(solution)/shard_map/ppermute | solution.py:86
  297.4 15.9 %collective-permute-start.40 = (bf16[2,624,128]{2,1,0:T(8,128)(2,1)}, bf16[2,624,128]{2,1,0:T(8,128)(2,1)S(1)}, u32[]{:S(2)}, u32[]{:S(2)}) collective-permute-start(bf16[2,624,128]{2,1,0:T(8,128)(2,1)} %get-tuple-element.51), channel_id=1, source_target_pairs={{0,1},{1,0},{2,3},{3,2},{4,5},{5,4},{6,7},{7,6},{8,9},{9,8},{10,11... | collective-permute-start | bytes 958472 | tf_op jit(solution)/shard_map/ppermute | solution.py:86
  299.5 16.8 %collective-permute-start.42 = (bf16[2,624,128]{2,1,0:T(8,128)(2,1)S(1)}, bf16[2,624,128]{2,1,0:T(8,128)(2,1)S(1)}, u32[]{:S(2)}, u32[]{:S(2)}) collective-permute-start(bf16[2,624,128]{2,1,0:T(8,128)(2,1)S(1)} %copy-done.81), channel_id=1, source_target_pairs={{0,1},{1,0},{2,3},{3,2},{4,5},{5,4},{6,7},{7,6},{8,9},{9,8},{10,11... | collective-permute-start | bytes 958472 | tf_op jit(solution)/shard_map/ppermute | solution.py:86
  299.6 15.5 %collective-permute-start.51 = (bf16[2,624,128]{2,1,0:T(8,128)(2,1)S(1)}, bf16[2,624,128]{2,1,0:T(8,128)(2,1)S(1)}, u32[]{:S(2)}, u32[]{:S(2)}) collective-permute-start(bf16[2,624,128]{2,1,0:T(8,128)(2,1)S(1)} %copy-done.82), channel_id=1, source_target_pairs={{0,1},{1,0},{2,3},{3,2},{4,5},{5,4},{6,7},{7,6},{8,9},{9,8},{10,11... | collective-permute-start | bytes 958472 | tf_op jit(solution)/shard_map/ppermute | solution.py:86
  300.0 13.6 %collective-permute-start.48 = (bf16[2,624,128]{2,1,0:T(8,128)(2,1)}, bf16[2,624,128]{2,1,0:T(8,128)(2,1)S(1)}, u32[]{:S(2)}, u32[]{:S(2)}) collective-permute-start(bf16[2,624,128]{2,1,0:T(8,128)(2,1)} %get-tuple-element.59), channel_id=1, source_target_pairs={{0,1},{1,0},{2,3},{3,2},{4,5},{5,4},{6,7},{7,6},{8,9},{9,8},{10,11... | collective-permute-start | bytes 958472 | tf_op jit(solution)/shard_map/ppermute | solution.py:86
  312.7 11.0 %collective-permute-start.47 = (bf16[2,624,128]{2,1,0:T(8,128)(2,1)S(1)}, bf16[2,624,128]{2,1,0:T(8,128)(2,1)S(1)}, u32[]{:S(2)}, u32[]{:S(2)}) collective-permute-start(bf16[2,624,128]{2,1,0:T(8,128)(2,1)S(1)} %copy-done.80), channel_id=1, source_target_pairs={{0,1},{1,0},{2,3},{3,2},{4,5},{5,4},{6,7},{7,6},{8,9},{9,8},{10,11... | collective-permute-start | bytes 958472 | tf_op jit(solution)/shard_map/ppermute | solution.py:86
  313.3 11.6 %collective-permute-start.59 = (bf16[2,1312,128]{2,1,0:T(8,128)(2,1)}, bf16[2,1312,128]{2,1,0:T(8,128)(2,1)S(1)}, u32[]{:S(2)}, u32[]{:S(2)}) collective-permute-start(bf16[2,1312,128]{2,1,0:T(8,128)(2,1)} %get-tuple-element.69), channel_id=1, source_target_pairs={{0,1},{1,0},{2,3},{3,2},{4,5},{5,4},{6,7},{7,6},{8,9},{9,8},{10,11... | collective-permute-start | bytes 2015240 | tf_op jit(solution)/shard_map/ppermute | solution.py:86
  313.6 9.9 %collective-permute-start.44 = (bf16[2,624,128]{2,1,0:T(8,128)(2,1)S(1)}, bf16[2,624,128]{2,1,0:T(8,128)(2,1)S(1)}, u32[]{:S(2)}, u32[]{:S(2)}) collective-permute-start(bf16[2,624,128]{2,1,0:T(8,128)(2,1)S(1)} %add_convert_fusion.14), channel_id=1, source_target_pairs={{0,2},{1,3},{2,0},{3,1},{4,6},{5,7},{6,4},{7,5},{8,10},{9,11},{10,... | collective-permute-start | bytes 958472 | tf_op jit(solution)/shard_map/ppermute | solution.py:86
  315.1 9.7 %collective-permute-start.49 = (bf16[2,624,128]{2,1,0:T(8,128)(2,1)S(1)}, bf16[2,624,128]{2,1,0:T(8,128)(2,1)S(1)}, u32[]{:S(2)}, u32[]{:S(2)}) collective-permute-start(bf16[2,624,128]{2,1,0:T(8,128)(2,1)S(1)} %add_convert_fusion.11), channel_id=1, source_target_pairs={{0,4},{1,5},{2,6},{3,7},{4,0},{5,1},{6,2},{7,3},{8,12},{9,13},{10,... | collective-permute-start | bytes 958472 | tf_op jit(solution)/shard_map/ppermute | solution.py:86
  316.3 41.7 %collective-permute-start.39 = (bf16[4,624,128]{2,1,0:T(8,128)(2,1)S(1)}, bf16[4,624,128]{2,1,0:T(8,128)(2,1)S(1)}, u32[]{:S(2)}, u32[]{:S(2)}) collective-permute-start(bf16[4,624,128]{2,1,0:T(8,128)(2,1)S(1)} %copy-done.79), channel_id=1, source_target_pairs={{0,1},{1,0},{2,3},{3,2},{4,5},{5,4},{6,7},{7,6},{8,9},{9,8},{10,11... | collective-permute-start | bytes 1916936 | tf_op jit(solution)/shard_map/ppermute | solution.py:86
  323.5 7.9 %collective-permute-start.58 = (bf16[2,1312,128]{2,1,0:T(8,128)(2,1)S(1)}, bf16[2,1312,128]{2,1,0:T(8,128)(2,1)S(1)}, u32[]{:S(2)}, u32[]{:S(2)}) collective-permute-start(bf16[2,1312,128]{2,1,0:T(8,128)(2,1)S(1)} %copy-done.75), channel_id=1, source_target_pairs={{0,1},{1,0},{2,3},{3,2},{4,5},{5,4},{6,7},{7,6},{8,9},{9,8},{10,11... | collective-permute-start | bytes 2015240 | tf_op jit(solution)/shard_map/ppermute | solution.py:86
  326.6 28.9 %collective-permute-start.63 = (bf16[2,1312,128]{2,1,0:T(8,128)(2,1)S(1)}, bf16[2,1312,128]{2,1,0:T(8,128)(2,1)S(1)}, u32[]{:S(2)}, u32[]{:S(2)}) collective-permute-start(bf16[2,1312,128]{2,1,0:T(8,128)(2,1)S(1)} %copy-done.74), channel_id=1, source_target_pairs={{0,1},{1,0},{2,3},{3,2},{4,5},{5,4},{6,7},{7,6},{8,9},{9,8},{10,11... | collective-permute-start | bytes 2015240 | tf_op jit(solution)/shard_map/ppermute | solution.py:86
  328.5 17.1 %collective-permute-start.60 = (bf16[2,1312,128]{2,1,0:T(8,128)(2,1)S(1)}, bf16[2,1312,128]{2,1,0:T(8,128)(2,1)S(1)}, u32[]{:S(2)}, u32[]{:S(2)}) collective-permute-start(bf16[2,1312,128]{2,1,0:T(8,128)(2,1)S(1)} %add_convert_fusion.6), channel_id=1, source_target_pairs={{0,2},{1,3},{2,0},{3,1},{4,6},{5,7},{6,4},{7,5},{8,10},{9,11},{10,... | collective-permute-start | bytes 2015240 | tf_op jit(solution)/shard_map/ppermute | solution.py:86
  330.0 26.4 %collective-permute-start.65 = (bf16[2,1312,128]{2,1,0:T(8,128)(2,1)S(1)}, bf16[2,1312,128]{2,1,0:T(8,128)(2,1)S(1)}, u32[]{:S(2)}, u32[]{:S(2)}) collective-permute-start(bf16[2,1312,128]{2,1,0:T(8,128)(2,1)S(1)} %add_convert_fusion.3), channel_id=1, source_target_pairs={{0,4},{1,5},{2,6},{3,7},{4,0},{5,1},{6,2},{7,3},{8,12},{9,13},{10,... | collective-permute-start | bytes 2015240 | tf_op jit(solution)/shard_map/ppermute | solution.py:86
  331.4 43.1 %collective-permute-start.55 = (bf16[4,1312,128]{2,1,0:T(8,128)(2,1)S(1)}, bf16[4,1312,128]{2,1,0:T(8,128)(2,1)S(1)}, u32[]{:S(2)}, u32[]{:S(2)}) collective-permute-start(bf16[4,1312,128]{2,1,0:T(8,128)(2,1)S(1)} %copy-done.73), channel_id=1, source_target_pairs={{0,1},{1,0},{2,3},{3,2},{4,5},{5,4},{6,7},{7,6},{8,9},{9,8},{10,11... | collective-permute-start | bytes 4030472 | tf_op jit(solution)/shard_map/ppermute | solution.py:86
  345.6 8.7 %collective-permute-start.41 = (bf16[2,624,128]{2,1,0:T(8,128)(2,1)S(1)}, bf16[2,624,128]{2,1,0:T(8,128)(2,1)S(1)}, u32[]{:S(2)}, u32[]{:S(2)}) collective-permute-start(bf16[2,624,128]{2,1,0:T(8,128)(2,1)S(1)} %add_convert_fusion.15), channel_id=1, source_target_pairs={{0,2},{1,3},{2,0},{3,1},{4,6},{5,7},{6,4},{7,5},{8,10},{9,11},{10,... | collective-permute-start | bytes 958472 | tf_op jit(solution)/shard_map/ppermute | solution.py:86
  354.4 10.5 %collective-permute-start.52 = (bf16[2,624,128]{2,1,0:T(8,128)(2,1)S(1)}, bf16[2,624,128]{2,1,0:T(8,128)(2,1)S(1)}, u32[]{:S(2)}, u32[]{:S(2)}) collective-permute-start(bf16[2,624,128]{2,1,0:T(8,128)(2,1)S(1)} %add_convert_fusion.9), channel_id=1, source_target_pairs={{0,4},{1,5},{2,6},{3,7},{4,0},{5,1},{6,2},{7,3},{8,12},{9,13},{10,... | collective-permute-start | bytes 958472 | tf_op jit(solution)/shard_map/ppermute | solution.py:86
  355.5 16.2 %collective-permute-start.45 = (bf16[2,624,128]{2,1,0:T(8,128)(2,1)S(1)}, bf16[2,624,128]{2,1,0:T(8,128)(2,1)S(1)}, u32[]{:S(2)}, u32[]{:S(2)}) collective-permute-start(bf16[2,624,128]{2,1,0:T(8,128)(2,1)S(1)} %add_convert_fusion.13), channel_id=1, source_target_pairs={{0,4},{1,5},{2,6},{3,7},{4,0},{5,1},{6,2},{7,3},{8,12},{9,13},{10,... | collective-permute-start | bytes 958472 | tf_op jit(solution)/shard_map/ppermute | solution.py:86
  356.4 16.4 %collective-permute-start.50 = (bf16[2,624,128]{2,1,0:T(8,128)(2,1)S(1)}, bf16[2,624,128]{2,1,0:T(8,128)(2,1)S(1)}, u32[]{:S(2)}, u32[]{:S(2)}) collective-permute-start(bf16[2,624,128]{2,1,0:T(8,128)(2,1)S(1)} %add_convert_fusion.10), channel_id=1, source_target_pairs={{0,2},{1,3},{2,0},{3,1},{4,6},{5,7},{6,4},{7,5},{8,10},{9,11},{10,... | collective-permute-start | bytes 958472 | tf_op jit(solution)/shard_map/ppermute | solution.py:86
  358.0 23.3 %collective-permute-start.57 = (bf16[2,1312,128]{2,1,0:T(8,128)(2,1)S(1)}, bf16[2,1312,128]{2,1,0:T(8,128)(2,1)S(1)}, u32[]{:S(2)}, u32[]{:S(2)}) collective-permute-start(bf16[2,1312,128]{2,1,0:T(8,128)(2,1)S(1)} %add_convert_fusion.7), channel_id=1, source_target_pairs={{0,2},{1,3},{2,0},{3,1},{4,6},{5,7},{6,4},{7,5},{8,10},{9,11},{10,... | collective-permute-start | bytes 2015240 | tf_op jit(solution)/shard_map/ppermute | solution.py:86
  364.8 21.2 %collective-permute-start.68 = (bf16[2,1312,128]{2,1,0:T(8,128)(2,1)S(1)}, bf16[2,1312,128]{2,1,0:T(8,128)(2,1)S(1)}, u32[]{:S(2)}, u32[]{:S(2)}) collective-permute-start(bf16[2,1312,128]{2,1,0:T(8,128)(2,1)S(1)} %add_convert_fusion.1), channel_id=1, source_target_pairs={{0,4},{1,5},{2,6},{3,7},{4,0},{5,1},{6,2},{7,3},{8,12},{9,13},{10,... | collective-permute-start | bytes 2015240 | tf_op jit(solution)/shard_map/ppermute | solution.py:86
  371.7 26.1 %collective-permute-start.61 = (bf16[2,1312,128]{2,1,0:T(8,128)(2,1)S(1)}, bf16[2,1312,128]{2,1,0:T(8,128)(2,1)S(1)}, u32[]{:S(2)}, u32[]{:S(2)}) collective-permute-start(bf16[2,1312,128]{2,1,0:T(8,128)(2,1)S(1)} %add_convert_fusion.5), channel_id=1, source_target_pairs={{0,4},{1,5},{2,6},{3,7},{4,0},{5,1},{6,2},{7,3},{8,12},{9,13},{10,... | collective-permute-start | bytes 2015240 | tf_op jit(solution)/shard_map/ppermute | solution.py:86
  372.8 25.0 %collective-permute-start.66 = (bf16[2,1312,128]{2,1,0:T(8,128)(2,1)S(1)}, bf16[2,1312,128]{2,1,0:T(8,128)(2,1)S(1)}, u32[]{:S(2)}, u32[]{:S(2)}) collective-permute-start(bf16[2,1312,128]{2,1,0:T(8,128)(2,1)S(1)} %add_convert_fusion.2), channel_id=1, source_target_pairs={{0,2},{1,3},{2,0},{3,1},{4,6},{5,7},{6,4},{7,5},{8,10},{9,11},{10,... | collective-permute-start | bytes 2015240 | tf_op jit(solution)/shard_map/ppermute | solution.py:86
  374.5 27.6 %collective-permute-start.54 = (bf16[624,128]{1,0:T(8,128)(2,1)S(1)}, bf16[624,128]{1,0:T(8,128)(2,1)S(1)}, u32[]{:S(2)}, u32[]{:S(2)}) collective-permute-start(bf16[624,128]{1,0:T(8,128)(2,1)S(1)} %get-tuple-element.152), channel_id=1, source_target_pairs={{0,24},{1,25},{2,26},{3,27},{4,28},{5,29},{6,30},{7,31},{8,16},{9,... | collective-permute-start | bytes 479240 | tf_op jit(solution)/shard_map/ppermute | solution.py:86
  381.3 21.9 %collective-permute-start.53 = (bf16[624,128]{1,0:T(8,128)(2,1)S(1)}, bf16[624,128]{1,0:T(8,128)(2,1)S(1)}, u32[]{:S(2)}, u32[]{:S(2)}) collective-permute-start(bf16[624,128]{1,0:T(8,128)(2,1)S(1)} %get-tuple-element.151), channel_id=1, source_target_pairs={{0,16},{1,17},{2,18},{3,19},{4,20},{5,21},{6,22},{7,23},{8,24},{9,... | collective-permute-start | bytes 479240 | tf_op jit(solution)/shard_map/ppermute | solution.py:86
  386.1 17.1 %collective-permute-start.46 = (bf16[624,128]{1,0:T(8,128)(2,1)S(1)}, bf16[624,128]{1,0:T(8,128)(2,1)S(1)}, u32[]{:S(2)}, u32[]{:S(2)}) collective-permute-start(bf16[624,128]{1,0:T(8,128)(2,1)S(1)} %get-tuple-element.149), channel_id=1, source_target_pairs={{0,8},{1,9},{2,10},{3,11},{4,12},{5,13},{6,14},{7,15},{8,0},{9,1},... | collective-permute-start | bytes 479240 | tf_op jit(solution)/shard_map/ppermute | solution.py:86
  398.6 12.8 %collective-permute-start.70 = (bf16[1312,128]{1,0:T(8,128)(2,1)S(1)}, bf16[1312,128]{1,0:T(8,128)(2,1)S(1)}, u32[]{:S(2)}, u32[]{:S(2)}) collective-permute-start(bf16[1312,128]{1,0:T(8,128)(2,1)S(1)} %get-tuple-element.148), channel_id=1, source_target_pairs={{0,24},{1,25},{2,26},{3,27},{4,28},{5,29},{6,30},{7,31},{8,16},{9,... | collective-permute-start | bytes 1007624 | tf_op jit(solution)/shard_map/ppermute | solution.py:86
  400.7 28.3 %collective-permute-start.69 = (bf16[1312,128]{1,0:T(8,128)(2,1)S(1)}, bf16[1312,128]{1,0:T(8,128)(2,1)S(1)}, u32[]{:S(2)}, u32[]{:S(2)}) collective-permute-start(bf16[1312,128]{1,0:T(8,128)(2,1)S(1)} %get-tuple-element.147), channel_id=1, source_target_pairs={{0,16},{1,17},{2,18},{3,19},{4,20},{5,21},{6,22},{7,23},{8,24},{9,... | collective-permute-start | bytes 1007624 | tf_op jit(solution)/shard_map/ppermute | solution.py:86
  402.2 26.8 %collective-permute-start.62 = (bf16[1312,128]{1,0:T(8,128)(2,1)S(1)}, bf16[1312,128]{1,0:T(8,128)(2,1)S(1)}, u32[]{:S(2)}, u32[]{:S(2)}) collective-permute-start(bf16[1312,128]{1,0:T(8,128)(2,1)S(1)} %get-tuple-element.145), channel_id=1, source_target_pairs={{0,8},{1,9},{2,10},{3,11},{4,12},{5,13},{6,14},{7,15},{8,0},{9,1},... | collective-permute-start | bytes 1007624 | tf_op jit(solution)/shard_map/ppermute | solution.py:86
  433.5 7.4 %collective-permute-start.72 = (f32[]{:T(128)}, f32[]{:T(128)}, u32[]{:S(2)}, u32[]{:S(2)}) collective-permute-start(f32[]{:T(128)} %add.565), channel_id=1, source_target_pairs={{0,2},{1,3},{2,0},{3,1},{4,6},{5,7},{6,4},{7,5},{8,10},{9,11},{10,... | collective-permute-start | bytes 20 | tf_op jit(solution)/shard_map/ppermute | solution.py:86
  436.2 5.4 %collective-permute-start.73 = (f32[]{:T(128)}, f32[]{:T(128)}, u32[]{:S(2)}, u32[]{:S(2)}) collective-permute-start(f32[]{:T(128)} %add.565), channel_id=1, source_target_pairs={{0,4},{1,5},{2,6},{3,7},{4,0},{5,1},{6,2},{7,3},{8,12},{9,13},{10,... | collective-permute-start | bytes 20 | tf_op jit(solution)/shard_map/ppermute | solution.py:86
  444.3 8.3 %collective-permute-start.75 = (f32[]{:T(128)}, f32[]{:T(128)}, u32[]{:S(2)}, u32[]{:S(2)}) collective-permute-start(f32[]{:T(128)} %add.568), channel_id=1, source_target_pairs={{0,8},{1,9},{2,10},{3,11},{4,12},{5,13},{6,14},{7,15},{8,0},{9,1},... | collective-permute-start | bytes 20 | tf_op jit(solution)/shard_map/ppermute | solution.py:86
  445.7 7.6 %collective-permute-start.76 = (f32[]{:T(128)}, f32[]{:T(128)}, u32[]{:S(2)}, u32[]{:S(2)}) collective-permute-start(f32[]{:T(128)} %add.568), channel_id=1, source_target_pairs={{0,16},{1,17},{2,18},{3,19},{4,20},{5,21},{6,22},{7,23},{8,24},{9,... | collective-permute-start | bytes 20 | tf_op jit(solution)/shard_map/ppermute | solution.py:86
  449.9 5.4 %collective-permute-start.77 = (f32[]{:T(128)}, f32[]{:T(128)}, u32[]{:S(2)}, u32[]{:S(2)}) collective-permute-start(f32[]{:T(128)} %add.568), channel_id=1, source_target_pairs={{0,24},{1,25},{2,26},{3,27},{4,28},{5,29},{6,30},{7,31},{8,16},{9,... | collective-permute-start | bytes 20 | tf_op jit(solution)/shard_map/ppermute | solution.py:86
  (102 other events, 825.8 us)

commit v2 on v1

--- a/solution.py
+++ b/solution.py
@@ -123,32 +123,28 @@
 
 
 def piece_slots(me):
-    order = []
+    slots = []
     for core in (0, 1):
-        order += [
-            (core, 0, 0, 0, 4),
-            (core, 0, 1, 0, 2),
-            (core, 0, 1, 2, 2),
-            (core, 1, 0, 0, 2),
-            (core, 1, 0, 2, 2),
-            (core, 1, 1, 0, 2),
-            (core, 1, 1, 2, 2),
-        ]
-    slots = []
-    for core, y, x, z, n in order:
-        slots.append([me ^ (core + 2 * x + 4 * y + 8 * (z + k)) for k in range(n)])
+        for across, first, n in ((0, 0, 4), (1, 0, 4), (2, 0, 4), (3, 0, 2), (3, 2, 2)):
+            slots.append([me ^ (core + 2 * across + 8 * (first + k)) for k in range(n)])
     return slots
 
 
-def gather_pieces(block):
-    zs = [block] + [swap(block, bit) for bit in ZBITS]
-    low_half = jnp.stack(zs[:2])
-    high_half = jnp.stack(zs[2:])
-    x_low, x_high = swap(low_half, XBIT), swap(high_half, XBIT)
-    y_low, y_high = swap(low_half, YBIT), swap(high_half, YBIT)
-    d_low, d_high = swap(y_low, XBIT), swap(x_high, YBIT)
-    own = [jnp.concatenate([low_half, high_half]), x_low, x_high, y_low, y_high, d_low, d_high]
-    return own + [swap(piece, CORE) for piece in own]
+def after(value, *others):
+    return lax.optimization_barrier((value, others))[0]
+
+
+def gather_along(block):
+    return [block] + [swap(block, bit) for bit in ZBITS]
+
+
+def gather_across(line):
+    x, y = swap(line, XBIT), swap(line, YBIT)
+    return line, x, y
+
+
+def gather_diagonal(x, y):
+    return swap(y[:2], XBIT), swap(x[2:], YBIT)
 
 
 def low_sum(*terms):
@@ -158,18 +154,30 @@
     return total.astype(jnp.bfloat16)
 
 
-def scatter_pieces(pieces):
-    got = [swap(piece, CORE) for piece in pieces[7:]]
-    own, x_low, x_high, y_low, y_high, d_low, d_high = pieces[:7]
-    d_low = swap(low_sum(d_low, got[5]), XBIT)
-    d_high = swap(low_sum(d_high, got[6]), YBIT)
-    x_low = swap(low_sum(x_low, got[1]), XBIT)
-    y_high = swap(low_sum(y_high, got[4]), YBIT)
-    x_high = swap(low_sum(x_high, got[2], d_high), XBIT)
-    y_low = swap(low_sum(y_low, got[3], d_low), YBIT)
-    low_half = low_sum(own[:2], got[0][:2], x_low, y_low)
-    high_half = low_sum(own[2:], got[0][2:], x_high, y_high)
-    zs = [low_half[0], low_half[1], high_half[0], high_half[1]]
+def scatter_core(pieces):
+    half = len(pieces) // 2
+    got = [swap(piece, CORE) for piece in reversed(pieces[half:])][::-1]
+    return [low_sum(piece, other) for piece, other in zip(pieces[:half], got)]
+
+
+def scatter_diagonal(sums):
+    return swap(sums[3], XBIT), swap(sums[4], YBIT)
+
+
+def scatter_across(sums, diagonal):
+    line, x, y = sums[:3]
+    d_low, d_high = diagonal
+    x = swap(jnp.concatenate([x[:2], low_sum(x[2:], d_high)]), XBIT)
+    y = swap(jnp.concatenate([low_sum(y[:2], d_low), y[2:]]), YBIT)
+    return x, y
+
+
+def scatter_line(sums, across):
+    line = low_sum(sums[0], *across)
+    return [line[k] for k in range(4)]
+
+
+def scatter_along(zs):
     total = zs[0].astype(jnp.float32)
     for value, bit in zip(zs[1:], ZBITS):
         total = total + swap(value, bit).astype(jnp.float32)
@@ -177,7 +185,7 @@
 
 
 def unflatten_kernel(shard, cols, me_ref, *refs):
-    pieces, (w_ref, v_ref), (stage, flat, sems) = refs[:14], refs[14:16], refs[16:]
+    pieces, (w_ref, v_ref), (stage, flat, sems) = refs[:10], refs[10:12], refs[12:]
     count, rows = stage.shape[0], stage.shape[1]
     me = me_ref[0]
     for piece, slots in zip(pieces, piece_slots(me)):
@@ -215,7 +223,7 @@
             jax.ShapeDtypeStruct((D, cols * LANES), jnp.bfloat16),
             jax.ShapeDtypeStruct((whole - D * cols, LANES), jnp.float32),
         ),
-        in_specs=[pl.BlockSpec(memory_space=pltpu.SMEM)] + [pl.BlockSpec(memory_space=pl.ANY)] * 14,
+        in_specs=[pl.BlockSpec(memory_space=pltpu.SMEM)] + [pl.BlockSpec(memory_space=pl.ANY)] * len(pieces),
         out_specs=(pl.BlockSpec(memory_space=pltpu.VMEM), pl.BlockSpec(memory_space=pltpu.VMEM)),
         scratch_shapes=[
             pltpu.VMEM((32, rows, LANES), jnp.bfloat16),
@@ -229,7 +237,7 @@
 def flatten_kernel(shard, widths, me_ref, *refs):
     n_in = len(widths)
     mats, v_ref = refs[:n_in], refs[n_in]
-    pieces, (stage, flat, sems) = refs[n_in + 1 : n_in + 15], refs[n_in + 15 :]
+    pieces, (stage, flat, sems) = refs[n_in + 1 : n_in + 11], refs[n_in + 11 :]
     count, rows = stage.shape[0], stage.shape[1]
     cols = sum(widths)
     me = me_ref[0]
@@ -280,36 +288,46 @@
     )(jnp.reshape(me, (1,)), *mats, vec_rows)
 
 
-def gather_weights(values, device, cols, vec_cols):
-    shard = values.shape[0]
-    count = lax.axis_size("sent")
-    if is_grid(count, shard):
-        pieces = gather_pieces(pack_shard(values, device))
-        mats, vec_rows = unflatten(pieces, device, shard, cols)
-        return mats, vec_rows.reshape(D, vec_cols)
-    full = lax.all_gather(values.astype(jnp.bfloat16), "sent", axis=0, tiled=True)
-    split = D * cols * LANES
-    vecs = full[split:].reshape(D, vec_cols).astype(jnp.float32)
-    return full[:split].reshape(D, cols * LANES), vecs
-
-
-def scatter_grads(mats, vecs, device, shard):
-    count = lax.axis_size("sent")
-    if is_grid(count, shard):
-        pieces = flatten([m.astype(jnp.bfloat16) for m in mats], vecs.reshape(-1, LANES), device, shard)
-        return unpack_shard(scatter_pieces(list(pieces)), device, shard)
-    flat = jnp.concatenate([jnp.concatenate(mats, axis=1).reshape(-1), vecs.reshape(-1)])
-    return lax.psum_scatter(flat, "sent", scatter_dimension=0, tiled=True)
+def gather_weights(attn_values, head_values, device):
+    shards = (attn_values.shape[0], head_values.shape[0])
+    if is_grid(lax.axis_size("sent"), *shards):
+        attn_zs = gather_along(pack_shard(attn_values, device))
+        head_block = after(pack_shard(head_values, device), attn_zs[1])
+        attn_line, attn_x, attn_y = gather_across(jnp.stack(attn_zs))
+        head_zs = gather_along(head_block)
+        attn_diagonal = gather_diagonal(attn_x, attn_y)
+        attn_own = (attn_line, attn_x, attn_y) + attn_diagonal
+        attn_pieces = attn_own + tuple(swap(piece, CORE) for piece in attn_own)
+        head_line, _ = lax.optimization_barrier((jnp.stack(head_zs), attn_diagonal))
+        head_line, head_x, head_y = gather_across(head_line)
+        head_own = (head_line, head_x, head_y) + gather_diagonal(head_x, head_y)
+        head_pieces = head_own + tuple(swap(piece, CORE) for piece in head_own)
+        attn_mats, attn_rows = unflatten(attn_pieces, device, shards[0], 24)
+        head_mats, head_rows = unflatten(head_pieces, device, shards[1], 54)
+        return attn_mats, attn_rows.reshape(D, 8 + POS), head_mats, head_rows.reshape(D, 8)
+    found = []
+    for values, cols, vec_cols in ((attn_values, 24, 8 + POS), (head_values, 54, 8)):
+        full = lax.all_gather(values.astype(jnp.bfloat16), "sent", axis=0, tiled=True)
+        split = D * cols * LANES
+        found.append(full[:split].reshape(D, cols * LANES))
+        found.append(full[split:].reshape(D, vec_cols).astype(jnp.float32))
+    return tuple(found)
 
 
 def gather_small(value, device):
     count = lax.axis_size("sent")
     if count != 32:
         return lax.all_gather(value, "sent", axis=0)
-    got = jnp.stack([value, swap(value, CORE)])
-    got = jnp.concatenate([got] + [swap(got, bit) for bit in (XBIT, YBIT, XBIT | YBIT)])
-    got = jnp.concatenate([got] + [swap(got, bit) for bit in ZBITS])
+    got = jnp.stack([value] + [swap(value, bit) for bit in ZBITS])
+    got = jnp.stack([got] + [swap(got, bit) for bit in (XBIT, YBIT, XBIT | YBIT)])
+    got = jnp.stack([got, swap(got, CORE)])
+    got = jnp.transpose(got, (2, 1, 0, 3, 4)).reshape((count,) + value.shape)
     return jnp.take(got, jnp.arange(count) ^ device, axis=0)
+
+
+def scatter_flat(mats, vecs):
+    flat = jnp.concatenate([jnp.concatenate(mats, axis=1).reshape(-1), vecs.reshape(-1)])
+    return lax.psum_scatter(flat, "sent", scatter_dimension=0, tiled=True)
 
 
 def sum_small(value):
@@ -341,8 +359,7 @@
     slot_count = lengths.shape[0]
     all_rows = 2 * tok_rows
     device = lax.axis_index("sent")
-    attn_mats, attn_vecs = gather_weights(attn_params, device, 24, 8 + POS)
-    head_mats, head_vecs = gather_weights(head_params, device, 54, 8)
+    attn_mats, attn_vecs, head_mats, head_vecs = gather_weights(attn_params, head_params, device)
     attn_vecs_low = attn_vecs.astype(jnp.bfloat16)
     w_qkv = attn_mats[:, : 3 * D]
     w_out = attn_mats[:, 3 * D :]
@@ -481,13 +498,29 @@
         ],
         axis=1,
     )
-    head_share = scatter_grads([g_up, g_down, g_pool], head_vec_grad, device, head_params.shape[0])
+    shards = (attn_params.shape[0], head_params.shape[0])
+    on_grid = is_grid(lax.axis_size("sent"), *shards)
+    head_mat_grads = [g_up, g_down, g_pool]
+    if on_grid:
+        head_pieces = flatten(
+            [m.astype(jnp.bfloat16) for m in head_mat_grads],
+            head_vec_grad.reshape(-1, LANES),
+            device,
+            shards[1],
+        )
+        d_first, head_pieces = lax.optimization_barrier((d_first, head_pieces))
+        head_sums = scatter_core(head_pieces)
+    else:
+        head_share = scatter_flat(head_mat_grads, head_vec_grad)
     d_first_res, g_gain_one, g_shift_one = first_back(d_first)
     d_branch = d_first_res * keep_attn
     g_out_bias = jnp.sum(d_branch, axis=0)
     branch_low = d_branch.astype(jnp.bfloat16)
     g_out = rows_dot(mixed_low, branch_low)
     d_mixed = target_dot_terms(branch_low, w_out).astype(jnp.bfloat16).reshape(-1, block, H, HD)
+    if on_grid:
+        d_mixed, head_sums = lax.optimization_barrier((d_mixed, head_sums))
+        head_diagonal = scatter_diagonal(head_sums)
     again = jnp.where(
         allowed,
         jnp.einsum("bqhd,bkhd->bhqk", queries, keys_low, preferred_element_type=jnp.float32)
@@ -512,6 +545,9 @@
     g_q_bias = jnp.sum(d_queries.reshape(all_rows, D), axis=0)
     g_v_bias = jnp.sum(d_values.reshape(all_rows, D), axis=0)
     qkv_grad_low = d_qkv.astype(jnp.bfloat16)
+    if on_grid:
+        qkv_grad_low, head_diagonal = lax.optimization_barrier((qkv_grad_low, head_diagonal))
+        head_across = scatter_across(head_sums, head_diagonal)
     g_qkv = rows_dot(attn_in_low, qkv_grad_low)
     d_attn_in = d_first_res + target_dot_terms(qkv_grad_low, w_qkv)
     d_normed = jnp.sum(d_attn_in.reshape(2, tok_rows, D) * keep_masks[:, 0], axis=0)
@@ -543,7 +579,23 @@
         ],
         axis=1,
     )
-    attn_share = scatter_grads([g_qkv, g_out], attn_vec_grad, device, attn_params.shape[0])
+    attn_mat_grads = [g_qkv, g_out]
+    if on_grid:
+        attn_pieces = flatten(
+            [m.astype(jnp.bfloat16) for m in attn_mat_grads],
+            attn_vec_grad.reshape(-1, LANES),
+            device,
+            shards[0],
+        )
+        attn_pieces, head_across = lax.optimization_barrier((attn_pieces, head_across))
+        head_zs = scatter_line(head_sums, head_across)
+        attn_sums = scatter_core(attn_pieces)
+        attn_diagonal = scatter_diagonal(attn_sums)
+        attn_zs = scatter_line(attn_sums, scatter_across(attn_sums, attn_diagonal))
+        head_share = unpack_shard(scatter_along(head_zs), device, shards[1])
+        attn_share = unpack_shard(scatter_along(attn_zs), device, shards[0])
+    else:
+        attn_share = scatter_flat(attn_mat_grads, attn_vec_grad)
     squares = jnp.sum(attn_share * attn_share) + jnp.sum(head_share * head_share)
     total_squares = sum_small(squares)
     loss = loss_sum / jnp.sum(valid_everything)

time: 469 us -> 417 us (0.89)
  waiting for transfers between devices: 148 us -> 106 us
  starting transfers between devices: 93.3 us -> 66.4 us
  other arithmetic: 35.8 us -> 58 us
  matrix products: 87.3 us -> 77.8 us
    ppermute x78 -> x62, waiting for transfers between devices: 148 us -> 106 us  [swap(): return lax.ppermute(value, 'sent', [(i, i ^ bit) for i in range(count)])]
    ppermute x78 -> x62, starting transfers between devices: 93.3 us -> 66.4 us  [swap(): return lax.ppermute(value, 'sent', [(i, i ^ bit) for i in range(count)])]
    convert_element_type x14 -> x15, other arithmetic: 2.9 us -> 16 us  [low_sum(): return total.astype(jnp.bfloat16)]
    unnamed x182 -> x213, local copies, waits for them, and re-layouts: 15.9 us -> 11.1 us
  transfers between devices with their start and end apart: 78 -> 62, of which waited for: 31 -> 26; matrix products, arithmetic and copies ran while one was open for 12% -> 20% of each run, Pallas kernels for 4% -> 4%
where the time goes in v2:
time: 417 us; the launch traced here: 412 us
  waiting for transfers between devices  106 us (25%)
  matrix products  77.8 us (19%)
  starting transfers between devices  66.4 us (16%)
  other arithmetic  58 us (14%)
  local copies, waits for them, and re-layouts  51.3 us (12%)
  Pallas kernels  37.2 us (9%)
  between operations  15.6 us (4%)
    ppermute x62, waiting for transfers between devices, swap(): return lax.ppermute(value, 'sent', [(i, i ^ bit) for i in range(count)])  106 us
    ppermute x62, starting transfers between devices, swap(): return lax.ppermute(value, 'sent', [(i, i ^ bit) for i in range(count)])  66.4 us
    dot_general x7, matrix products, plain_dot(): return jnp.dot(left_op, right_op, preferred_element_type=jnp.float32)  20.9 us
    dot_general x6, matrix products, target_dot_terms(): lax.dot_general(left_op, right_op, (((1,), (1,)), ((), ())), preferred_el...  20.5 us
    pallas_call x2, Pallas kernels, unflatten(): pl.pallas_call(functools.partial(unflatten_kernel, shard, cols), out_shap...  20.1 us
    dot_general x6, matrix products, rows_dot(): lax.dot_general(left_op, right_op, (((0,), (0,)), ((), ())), preferred_el...  18.7 us
    pallas_call x2, Pallas kernels, flatten(): pl.pallas_call(functools.partial(flatten_kernel, shard, widths), out_shap...  17.1 us
    convert_element_type x15, other arithmetic, low_sum(): return total.astype(jnp.bfloat16)  16 us
  transfers between devices with their start and end apart: 62, of which 26 were waited for; matrix products, arithmetic and copies ran while one was open for 20% of the time, Pallas kernels for 4%

profile of v2, /device:TPU:0, one launch (start us, length us, event | category | flops | bytes accessed | tf_op | source)
XLA Modules:
  0.0 412.0 jit_solution(16047607362336959355)
XLA Ops:
  1.9 3.1 collective-permute-start
  5.0 2.5 collective-permute-start.2
  13.2 5.1 %convert_multiply_fusion = f32[2,3,256,768]{3,2,1,0:T(8,128)} fusion(s32[2,3,256,768]{3,2,1,0:T(8,128)} %param.15), kind=kLoop, calls=%fused_computation.10 | loop fusion | flops 2359296 | bytes 9437184 | tf_op jit(solution)/shard_map/div | solution.py:395
  25.6 2.7 collective-permute-start.14
  28.3 1.7 collective-permute-start.12
  30.0 4.5 %fusion.133 = (f32[2,1,256,768]{3,2,1,0:T(8,128)}, f32[2,1,256,768]{3,2,1,0:T(8,128)}, f32[2,1,256,768]{3,2,1,0:T(8,128)S(1)}) fusion(f32[2,3,256,768]{3,2,1,0:T(8,128)} %convert_multiply_fusion), kind=kLoop, calls=%fused_computation.285 | loop fusion | bytes 9437184 | tf_op jit(solution)/shard_map/slice | solution.py:396
  34.5 2.6 collective-permute-done.4.refs_2_
  41.7 14.3 %collective-permute-done.13 = bf16[1312,128]{1,0:T(8,128)(2,1)S(1)} collective-permute-done((bf16[1312,128]{1,0:T(8,128)(2,1)S(1)}, bf16[1312,128]{1,0:T(8,128)(2,1)S(1)}, u32[]{:S(2)}, u32[]{:S(2)}) %collective-permute-start.13) | collective-permute-done | bytes 335904 | tf_op jit(solution)/shard_map/ppermute | solution.py:86
  59.4 2.5 pad_maximum_fusion.1.refs_0_
  63.1 8.0 %shard_map.220 = (bf16[768,3072]{1,0:T(8,128)(2,1)}, f32[816,128]{1,0:T(8,128)}) custom-call(s32[1]{0:T(128)} %bitcast.1.me_ref, bf16[4,624,128]{2,1,0:T(8,128)(2,1)} %copy-done.25, bf16[4,624,128]{2,1,0:T(8,128)(2,1)} %copy-done.27, bf16[4,624,128]{2,1,0:T(8,128)(2,1)} %copy-done.26, bf16[2,624,128]{2,1,0:T(8,128)(2,1)} %collective-permute-done.5.refs_3_, ...), custom_call_target="tpu_custom_call" | custom-call | tf_op jit(solution)/shard_map/pallas_call | solution.py:220
  71.1 2.0 reshape.422
  79.5 2.0 fusion.1
  81.5 2.5 copy.72
  84.0 4.2 %reshape.423 = bf16[4,128,3,12,64]{1,0,4,3,2:T(4,128)(2,1)S(1)} reshape(bf16[512,2304]{0,1:T(8,128)(2,1)} %copy.72) | data formatting | bytes 4718592 | tf_op jit(solution)/shard_map/reshape | solution.py:402
  90.4 4.0 collective-permute-done.16.refs_2_
  101.5 10.4 %collective-permute-done.17.refs_3_ = bf16[2,1312,128]{2,1,0:T(8,128)(2,1)S(1)} collective-permute-done((bf16[2,1312,128]{2,1,0:T(8,128)(2,1)S(1)}, bf16[2,1312,128]{2,1,0:T(8,128)(2,1)S(1)}, u32[]{:S(2)}, u32[]{:S(2)}) %collective-permute-start.17) | collective-permute-done | bytes 671776 | tf_op jit(solution)/shard_map/ppermute | solution.py:86
  111.9 2.4 collective-permute-done.18.refs_4_
  114.4 2.5 fusion.138
  118.6 12.1 %shard_map.221 = (bf16[768,6912]{1,0:T(8,128)(2,1)}, f32[48,128]{1,0:T(8,128)}) custom-call(s32[1]{0:T(128)} %bitcast.1.me_ref, bf16[4,1312,128]{2,1,0:T(8,128)(2,1)} %pad_maximum_fusion.1.refs_0_, bf16[4,1312,128]{2,1,0:T(8,128)(2,1)} %collective-permute-done.15.refs_1_, bf16[4,1312,128]{2,1,0:T(8,128)(2,1)} %collective-permute-done.16.refs_2_, ...), custom_call_target="tpu_custom_call" | custom-call | tf_op jit(solution)/shard_map/pallas_call | solution.py:220
  132.8 6.7 %multiply_convert_fusion = (bf16[512,3072]{1,0:T(8,128)(2,1)S(1)}, f32[512,3072]{1,0:T(8,128)}) fusion(f32[3072]{0:T(1024)S(1)} %add.471, bf16[768,6912]{1,0:T(8,128)(2,1)} %get-tuple-element.74, f32[512,768]{1,0:T(8,128)S(1)} %get-tuple-element.208, f32[768]{0:T(1024)S(1)} %get-tuple-element.136, f32[768]{0:T(1024)S(1)} %get-tuple-element.135, ...), kind=kOutput, calls=%fused_computation.4 | convolution fusion | flops 2427322368 | bytes 15751168 | tf_op jit(solution)/shard_map/dot_general | solution.py:53
  139.6 6.4 %fusion.139 = (f32[512]{0:T(512)S(1)}, f32[512,768]{1,0:T(8,128)S(1)}) fusion(f32[768]{0:T(1024)S(1)} %get-tuple-element.146, bf16[512,3072]{1,0:T(8,128)(2,1)S(1)} %get-tuple-element.209, bf16[768,6912]{1,0:T(8,128)(2,1)} %get-tuple-element.74, f32[2,1,256,768]{3,2,1,0:T(8,128)S(1)} %copy-done.9, f32[768]{0:T(1024)S(1)} %get-tuple-element.136, ...), kind=kOutput, calls=%fused_computation.291 | convolution fusion | flops 2419064320 | bytes 12598272 | tf_op jit(solution)/shard_map/dot_general | solution.py:63
  149.2 1.7 gather_fusion
  152.8 2.8 collective-permute-start.26
  158.4 1.8 collective-permute-done.25
  164.4 1.7 collective-permute-done.29
  173.3 2.8 gather_fusion.1
  186.1 7.1 %fusion.141 = (f32[3072]{0:T(1024)S(1)}, bf16[512,3072]{1,0:T(8,128)(2,1)S(1)}) fusion(bf16[768,6912]{1,0:T(8,128)(2,1)} %get-tuple-element.74, bf16[512,768]{1,0:T(8,128)(2,1)S(1)} %get-tuple-element.174, f32[512,3072]{1,0:T(8,128)S(1)} %copy-done.103, f32[3072]{0:T(1024)S(1)} %copy-done.81), kind=kOutput, calls=%fused_computation.293 | convolution fusion | flops 2439508992 | bytes 14966784 | tf_op jit(solution)/shard_map/dot_general | solution.py:53
  193.3 5.0 %add_add_fusion.3 = f32[512,768]{1,0:T(8,128)S(1)} fusion(f32[512,768]{1,0:T(8,128)S(1)} %get-tuple-element.176, bf16[768,6912]{1,0:T(8,128)(2,1)} %get-tuple-element.74, bf16[512,3072]{1,0:T(8,128)(2,1)S(1)} %get-tuple-element.218, f32[512]{0:T(512)S(1)} %negate_multiply_fusion.1), kind=kOutput, calls=%fused_computation.81 | convolution fusion | flops 2416705536 | bytes 11012096 | tf_op jit(solution)/shard_map/dot_general | solution.py:63
  198.3 4.9 %convolution_convert_fusion.2.refs_0_ = bf16[768,3072]{1,0:T(8,128)(2,1)} fusion(bf16[512,3072]{1,0:T(8,128)(2,1)S(1)} %get-tuple-element.218, f32[512,768]{1,0:T(8,128)S(1)} %get-tuple-element.208, f32[768]{0:T(1024)S(1)} %copy-done.92, f32[768]{0:T(1024)S(1)} %get-tuple-element.135, f32[512]{0:T(512)S(1)} %copy-done.76, f32[512]{0:T(512)S(1)} %copy-done.66), kind=kOutput, calls=%fused_computation.8 | convolution fusion | flops 2420244480 | bytes 9447424 | tf_op jit(solution)/shard_map/dot_general | solution.py:57
  203.3 4.4 %convolution_convert_fusion.1.refs_1_ = bf16[768,3072]{1,0:T(8,128)(2,1)} fusion(bf16[512,3072]{1,0:T(8,128)(2,1)S(1)} %copy-done.105, bf16[512,768]{1,0:T(8,128)(2,1)S(1)} %get-tuple-element.174), kind=kOutput, calls=%fused_computation.7 | convolution fusion | flops 2418278400 | bytes 8650752 | tf_op jit(solution)/shard_map/dot_general | solution.py:57
  211.7 10.1 %shard_map.222 = (bf16[4,1312,128]{2,1,0:T(8,128)(2,1)}, bf16[4,1312,128]{2,1,0:T(8,128)(2,1)}, bf16[4,1312,128]{2,1,0:T(8,128)(2,1)}, bf16[2,1312,128]{2,1,0:T(...) custom-call(s32[1]{0:T(128)} %bitcast.1.me_ref, ...), custom_call_target="tpu_custom_call" | custom-call | tf_op jit(solution)/shard_map/pallas_call | solution.py:276
  224.5 2.2 convolution_convert_fusion.5
  226.7 1.8 convolution_convert_fusion.3.refs_1_
  231.7 2.4 add_convert_fusion.7
  234.1 2.1 add_convert_fusion.6
  237.7 2.9 add_convert_fusion.2
  242.2 2.2 fusion.72
  244.9 2.1 bitcast_reduce_fusion
  247.0 5.1 %fusion.57 = bf16[4,128,1,12,64]{1,4,3,0,2:T(8,128)(2,1)} fusion(f32[4,12,128,128]{2,3,1,0:T(8,128)} %fusion.72, f32[4,12,128,128]{2,3,1,0:T(8,128)S(1)} %copy-done.5, f32[4,12,128]{2,1,0:T(8,128)S(1)} %copy-done.59, bf16[4,128,1,12,64]{1,0,4,3,2:T(4,128)(2,1)} %copy-done.36), kind=kOutput, calls=%fused_computation.93 | convolution fusion | flops 106567808 | bytes 7888896 | tf_op jit(solution)/shard_map/bhqk,bqhd->bkhd/dot_general | solution.py:543
  252.1 5.2 %bitcast_reduce_fusion.1 = (f32[12,64]{1,0:T(8,128)S(1)}, bf16[4,12,64,128]{3,2,1,0:T(8,128)(2,1)}) fusion(f32[4,12,128,128]{2,3,1,0:T(8,128)} %fusion.72, f32[4,12,128,128]{2,3,1,0:T(8,128)S(1)} %copy-done.5, f32[4,12,128]{2,1,0:T(8,128)S(1)} %copy-done.59, bf16[4,128,1,12,64]{1,0,4,3,2:T(4,128)(2,1)} %copy-done.35), kind=kOutput, calls=%fused_computation.47 | convolution fusion | flops 106960256 | bytes 7891968 | tf_op jit(solution)/shard_map/bhqk,bkhd->bqhd/dot_general | solution.py:540
  261.1 2.4 copy.89
  263.6 1.9 copy.137
  265.6 9.3 %collective-permute-done.36 = bf16[2,1312,128]{2,1,0:T(8,128)(2,1)} collective-permute-done((bf16[2,1312,128]{2,1,0:T(8,128)(2,1)}, bf16[2,1312,128]{2,1,0:T(8,128)(2,1)}, u32[]{:S(2)}, u32[]{:S(2)}) %collective-permute-start.36) | collective-permute-done | bytes 671776 | tf_op jit(solution)/shard_map/ppermute | solution.py:86
  276.0 4.9 %fusion.32 = (f32[768]{0:T(1024)S(1)}, f32[512,768]{1,0:T(8,128)S(1)}) fusion(f32[2,1,256,768]{3,2,1,0:T(8,128)S(1)} %copy-done.8, bf16[512,2304]{0,1:T(8,128)(2,1)} %bitcast.214, bf16[768,3072]{1,0:T(8,128)(2,1)} %get-tuple-element.71, f32[512,768]{1,0:T(8,128)S(1)} %copy-done.12, f32[512]{0:T(512)S(1)} %negate_multiply_fusion), kind=kOutput, calls=%fused_computation.61 | convolution fusion | flops 1813511424 | bytes 10621952 | tf_op jit(solution)/shard_map/dot_general | solution.py:63
  281.0 1.8 fusion.28
  293.6 5.7 %convolution_convert_fusion.refs_0_ = bf16[768,2304]{1,0:T(8,128)(2,1)} fusion(bf16[512,768]{1,0:T(8,128)(2,1)} %copy-done.34, bf16[512,2304]{0,1:T(8,128)(2,1)} %bitcast.215), kind=kOutput, calls=%fused_computation.6 | convolution fusion | flops 1813708800 | bytes 6684672 | tf_op jit(solution)/shard_map/dot_general | solution.py:57
  299.3 7.0 %shard_map.223 = (bf16[4,624,128]{2,1,0:T(8,128)(2,1)}, bf16[4,624,128]{2,1,0:T(8,128)(2,1)}, bf16[4,624,128]{2,1,0:T(8,128)(2,1)}, bf16[2,624,128]{2,1,0:T(8,12...) custom-call(s32[1]{0:T(128)} %bitcast.1.me_ref, ...), custom_call_target="tpu_custom_call" | custom-call | tf_op jit(solution)/shard_map/pallas_call | solution.py:276
  306.3 11.0 %collective-permute-done.38 = bf16[4,1312,128]{2,1,0:T(8,128)(2,1)S(1)} collective-permute-done((bf16[4,1312,128]{2,1,0:T(8,128)(2,1)}, bf16[4,1312,128]{2,1,0:T(8,128)(2,1)S(1)}, u32[]{:S(2)}, u32[]{:S(2)}) %collective-permute-start.38) | collective-permute-done | bytes 1343520 | tf_op jit(solution)/shard_map/ppermute | solution.py:86
  317.4 3.2 collective-permute-done.39
  321.6 1.9 add_convert_fusion
  323.7 1.7 collective-permute-start.54
  330.1 6.4 %collective-permute-done.47 = bf16[2,624,128]{2,1,0:T(8,128)(2,1)S(1)} collective-permute-done((bf16[2,624,128]{2,1,0:T(8,128)(2,1)S(1)}, bf16[2,624,128]{2,1,0:T(8,128)(2,1)S(1)}, u32[]{:S(2)}, u32[]{:S(2)}) %collective-permute-start.47) | collective-permute-done | bytes 319520 | tf_op jit(solution)/shard_map/ppermute | solution.py:86
  337.5 7.9 %collective-permute-done.43 = bf16[2,624,128]{2,1,0:T(8,128)(2,1)S(1)} collective-permute-done((bf16[2,624,128]{2,1,0:T(8,128)(2,1)S(1)}, bf16[2,624,128]{2,1,0:T(8,128)(2,1)S(1)}, u32[]{:S(2)}, u32[]{:S(2)}) %collective-permute-start.43) | collective-permute-done | bytes 319520 | tf_op jit(solution)/shard_map/ppermute | solution.py:86
  347.6 8.4 %collective-permute-done.53 = bf16[1312,128]{1,0:T(8,128)(2,1)S(1)} collective-permute-done((bf16[1312,128]{1,0:T(8,128)(2,1)S(1)}, bf16[1312,128]{1,0:T(8,128)(2,1)S(1)}, u32[]{:S(2)}, u32[]{:S(2)}) %collective-permute-start.53) | collective-permute-done | bytes 335904 | tf_op jit(solution)/shard_map/ppermute | solution.py:86
  356.3 3.9 collective-permute-done.48
  362.6 4.6 %collective-permute-start.50 = (bf16[624,128]{1,0:T(8,128)(2,1)S(1)}, bf16[624,128]{1,0:T(8,128)(2,1)S(1)}, u32[]{:S(2)}, u32[]{:S(2)}) collective-permute-start(bf16[624,128]{1,0:T(8,128)(2,1)S(1)} %get-tuple-element.195), channel_id=1, source_target_pairs={{0,16},{1,17},{2,18},{3,19},{4,20},{5,21},{6,22},{7,23},{8,24},{9,... | collective-permute-start | bytes 479240 | tf_op jit(solution)/shard_map/ppermute | solution.py:86
  368.6 9.7 %collective-permute-done.50 = bf16[624,128]{1,0:T(8,128)(2,1)S(1)} collective-permute-done((bf16[624,128]{1,0:T(8,128)(2,1)S(1)}, bf16[624,128]{1,0:T(8,128)(2,1)S(1)}, u32[]{:S(2)}, u32[]{:S(2)}) %collective-permute-start.50) | collective-permute-done | bytes 159776 | tf_op jit(solution)/shard_map/ppermute | solution.py:86
  382.6 2.5 collective-permute-start.56
  385.1 2.1 collective-permute-start.57
  387.1 2.9 collective-permute-start.58
  394.3 4.0 collective-permute-start.60
  398.2 3.0 collective-permute-start.61
  405.0 2.5 multiply_add_fusion.7
  407.5 2.0 multiply_add_fusion.5
  (457 shorter events, 114.8 us)
Async XLA Ops:
  1.9 19.0 %collective-permute-start = (bf16[624,128]{1,0:T(8,128)(2,1)S(1)}, bf16[624,128]{1,0:T(8,128)(2,1)S(1)}, u32[]{:S(2)}, u32[]{:S(2)}) collective-permute-start(bf16[624,128]{1,0:T(8,128)(2,1)S(1)} %fusion.88), channel_id=1, source_target_pairs={{0,8},{1,9},{2,10},{3,11},{4,12},{5,13},{6,14},{7,15},{8,0},{9,1},... | collective-permute-start | bytes 479240 | tf_op jit(solution)/shard_map/ppermute | solution.py:86
  5.0 16.0 %collective-permute-start.2 = (bf16[624,128]{1,0:T(8,128)(2,1)S(1)}, bf16[624,128]{1,0:T(8,128)(2,1)S(1)}, u32[]{:S(2)}, u32[]{:S(2)}) collective-permute-start(bf16[624,128]{1,0:T(8,128)(2,1)S(1)} %fusion.88), channel_id=1, source_target_pairs={{0,24},{1,25},{2,26},{3,27},{4,28},{5,29},{6,30},{7,31},{8,16},{9,... | collective-permute-start | bytes 479240 | tf_op jit(solution)/shard_map/ppermute | solution.py:86
  7.5 14.2 %collective-permute-start.1 = (bf16[624,128]{1,0:T(8,128)(2,1)S(1)}, bf16[624,128]{1,0:T(8,128)(2,1)S(1)}, u32[]{:S(2)}, u32[]{:S(2)}) collective-permute-start(bf16[624,128]{1,0:T(8,128)(2,1)S(1)} %fusion.88), channel_id=1, source_target_pairs={{0,16},{1,17},{2,18},{3,19},{4,20},{5,21},{6,22},{7,23},{8,24},{9,... | collective-permute-start | bytes 479240 | tf_op jit(solution)/shard_map/ppermute | solution.py:86
  21.8 15.3 %collective-permute-start.4 = (bf16[4,624,128]{2,1,0:T(8,128)(2,1)S(1)}, bf16[4,624,128]{2,1,0:T(8,128)(2,1)S(1)}, u32[]{:S(2)}, u32[]{:S(2)}) collective-permute-start(bf16[4,624,128]{2,1,0:T(8,128)(2,1)S(1)} %pad_maximum_fusion.4.refs_0_), channel_id=1, source_target_pairs={{0,4},{1,5},{2,6},{3,7},{4,0},{5,1},{6,2},{7,3},{8,12},{9,13},{10,... | collective-permute-start | bytes 1916936 | tf_op jit(solution)/shard_map/ppermute | solution.py:86
  23.4 15.0 %collective-permute-start.3 = (bf16[4,624,128]{2,1,0:T(8,128)(2,1)S(1)}, bf16[4,624,128]{2,1,0:T(8,128)(2,1)S(1)}, u32[]{:S(2)}, u32[]{:S(2)}) collective-permute-start(bf16[4,624,128]{2,1,0:T(8,128)(2,1)S(1)} %pad_maximum_fusion.4.refs_0_), channel_id=1, source_target_pairs={{0,2},{1,3},{2,0},{3,1},{4,6},{5,7},{6,4},{7,5},{8,10},{9,11},{10,... | collective-permute-start | bytes 1916936 | tf_op jit(solution)/shard_map/ppermute | solution.py:86
  25.6 15.0 %collective-permute-start.14 = (bf16[1312,128]{1,0:T(8,128)(2,1)S(1)}, bf16[1312,128]{1,0:T(8,128)(2,1)S(1)}, u32[]{:S(2)}, u32[]{:S(2)}) collective-permute-start(bf16[1312,128]{1,0:T(8,128)(2,1)S(1)} %fusion.77), channel_id=1, source_target_pairs={{0,24},{1,25},{2,26},{3,27},{4,28},{5,29},{6,30},{7,31},{8,16},{9,... | collective-permute-start | bytes 1007624 | tf_op jit(solution)/shard_map/ppermute | solution.py:86
  28.3 27.7 %collective-permute-start.13 = (bf16[1312,128]{1,0:T(8,128)(2,1)S(1)}, bf16[1312,128]{1,0:T(8,128)(2,1)S(1)}, u32[]{:S(2)}, u32[]{:S(2)}) collective-permute-start(bf16[1312,128]{1,0:T(8,128)(2,1)S(1)} %fusion.77), channel_id=1, source_target_pairs={{0,16},{1,17},{2,18},{3,19},{4,20},{5,21},{6,22},{7,23},{8,24},{9,... | collective-permute-start | bytes 1007624 | tf_op jit(solution)/shard_map/ppermute | solution.py:86
  28.3 27.7 %collective-permute-start.12 = (bf16[1312,128]{1,0:T(8,128)(2,1)S(1)}, bf16[1312,128]{1,0:T(8,128)(2,1)S(1)}, u32[]{:S(2)}, u32[]{:S(2)}) collective-permute-start(bf16[1312,128]{1,0:T(8,128)(2,1)S(1)} %fusion.77), channel_id=1, source_target_pairs={{0,8},{1,9},{2,10},{3,11},{4,12},{5,13},{6,14},{7,15},{8,0},{9,1},... | collective-permute-start | bytes 1007624 | tf_op jit(solution)/shard_map/ppermute | solution.py:86
  37.1 24.8 %collective-permute-start.7 = (bf16[4,624,128]{2,1,0:T(8,128)(2,1)S(1)}, bf16[4,624,128]{2,1,0:T(8,128)(2,1)}, u32[]{:S(2)}, u32[]{:S(2)}) collective-permute-start(bf16[4,624,128]{2,1,0:T(8,128)(2,1)S(1)} %pad_maximum_fusion.4.refs_0_), channel_id=1, source_target_pairs={{0,1},{1,0},{2,3},{3,2},{4,5},{5,4},{6,7},{7,6},{8,9},{9,8},{10,11... | collective-permute-start | bytes 1916936 | tf_op jit(solution)/shard_map/ppermute | solution.py:86
  38.4 19.3 %collective-permute-start.5 = (bf16[2,624,128]{2,1,0:T(8,128)(2,1)}, bf16[2,624,128]{2,1,0:T(8,128)(2,1)}, u32[]{:S(2)}, u32[]{:S(2)}) collective-permute-start(bf16[2,624,128]{2,1,0:T(8,128)(2,1)} %slice.211), channel_id=1, source_target_pairs={{0,2},{1,3},{2,0},{3,1},{4,6},{5,7},{6,4},{7,5},{8,10},{9,11},{10,... | collective-permute-start | bytes 958472 | tf_op jit(solution)/shard_map/ppermute | solution.py:86
  40.6 17.5 %collective-permute-start.6 = (bf16[2,624,128]{2,1,0:T(8,128)(2,1)}, bf16[2,624,128]{2,1,0:T(8,128)(2,1)}, u32[]{:S(2)}, u32[]{:S(2)}) collective-permute-start(bf16[2,624,128]{2,1,0:T(8,128)(2,1)} %slice.212), channel_id=1, source_target_pairs={{0,4},{1,5},{2,6},{3,7},{4,0},{5,1},{6,2},{7,3},{8,12},{9,13},{10,... | collective-permute-start | bytes 958472 | tf_op jit(solution)/shard_map/ppermute | solution.py:86
  56.0 6.6 %collective-permute-start.8 = (bf16[4,624,128]{2,1,0:T(8,128)(2,1)S(1)}, bf16[4,624,128]{2,1,0:T(8,128)(2,1)}, u32[]{:S(2)}, u32[]{:S(2)}) collective-permute-start(bf16[4,624,128]{2,1,0:T(8,128)(2,1)S(1)} %collective-permute-done.3.refs_1_), channel_id=1, source_target_pairs={{0,1},{1,0},{2,3},{3,2},{4,5},{5,4},{6,7},{7,6},{8,9},{9,8},{10,11... | collective-permute-start | bytes 1916936 | tf_op jit(solution)/shard_map/ppermute | solution.py:86
  56.0 7.0 %collective-permute-start.9 = (bf16[4,624,128]{2,1,0:T(8,128)(2,1)S(1)}, bf16[4,624,128]{2,1,0:T(8,128)(2,1)}, u32[]{:S(2)}, u32[]{:S(2)}) collective-permute-start(bf16[4,624,128]{2,1,0:T(8,128)(2,1)S(1)} %collective-permute-done.4.refs_2_), channel_id=1, source_target_pairs={{0,1},{1,0},{2,3},{3,2},{4,5},{5,4},{6,7},{7,6},{8,9},{9,8},{10,11... | collective-permute-start | bytes 1916936 | tf_op jit(solution)/shard_map/ppermute | solution.py:86
  57.7 5.4 %collective-permute-start.10 = (bf16[2,624,128]{2,1,0:T(8,128)(2,1)}, bf16[2,624,128]{2,1,0:T(8,128)(2,1)}, u32[]{:S(2)}, u32[]{:S(2)}) collective-permute-start(bf16[2,624,128]{2,1,0:T(8,128)(2,1)} %collective-permute-done.5.refs_3_), channel_id=1, source_target_pairs={{0,1},{1,0},{2,3},{3,2},{4,5},{5,4},{6,7},{7,6},{8,9},{9,8},{10,11... | collective-permute-start | bytes 958472 | tf_op jit(solution)/shard_map/ppermute | solution.py:86
  58.1 5.0 %collective-permute-start.11 = (bf16[2,624,128]{2,1,0:T(8,128)(2,1)}, bf16[2,624,128]{2,1,0:T(8,128)(2,1)}, u32[]{:S(2)}, u32[]{:S(2)}) collective-permute-start(bf16[2,624,128]{2,1,0:T(8,128)(2,1)} %collective-permute-done.6.refs_4_), channel_id=1, source_target_pairs={{0,1},{1,0},{2,3},{3,2},{4,5},{5,4},{6,7},{7,6},{8,9},{9,8},{10,11... | collective-permute-start | bytes 958472 | tf_op jit(solution)/shard_map/ppermute | solution.py:86
  59.4 91.5 %copy-start.94 = (pred[16]{0:T(512)(128)(4,1)}, pred[16]{0:T(512)(128)(4,1)S(1)}, u32[]{:S(2)}) copy-start(pred[16]{0:T(512)(128)(4,1)S(1)} %broadcast_in_dim.142) | copy-start | bytes 52
  61.9 35.2 %collective-permute-start.15 = (bf16[4,1312,128]{2,1,0:T(8,128)(2,1)}, bf16[4,1312,128]{2,1,0:T(8,128)(2,1)}, u32[]{:S(2)}, u32[]{:S(2)}) collective-permute-start(bf16[4,1312,128]{2,1,0:T(8,128)(2,1)} %pad_maximum_fusion.1.refs_0_), channel_id=1, source_target_pairs={{0,2},{1,3},{2,0},{3,1},{4,6},{5,7},{6,4},{7,5},{8,10},{9,11},{10,... | collective-permute-start | bytes 4030472 | tf_op jit(solution)/shard_map/ppermute | solution.py:86
  62.5 31.8 %collective-permute-start.16 = (bf16[4,1312,128]{2,1,0:T(8,128)(2,1)}, bf16[4,1312,128]{2,1,0:T(8,128)(2,1)}, u32[]{:S(2)}, u32[]{:S(2)}) collective-permute-start(bf16[4,1312,128]{2,1,0:T(8,128)(2,1)} %pad_maximum_fusion.1.refs_0_), channel_id=1, source_target_pairs={{0,4},{1,5},{2,6},{3,7},{4,0},{5,1},{6,2},{7,3},{8,12},{9,13},{10,... | collective-permute-start | bytes 4030472 | tf_op jit(solution)/shard_map/ppermute | solution.py:86
  63.1 54.2 %collective-permute-start.19 = (bf16[4,1312,128]{2,1,0:T(8,128)(2,1)}, bf16[4,1312,128]{2,1,0:T(8,128)(2,1)}, u32[]{:S(2)}, u32[]{:S(2)}) collective-permute-start(bf16[4,1312,128]{2,1,0:T(8,128)(2,1)} %pad_maximum_fusion.1.refs_0_), channel_id=1, source_target_pairs={{0,1},{1,0},{2,3},{3,2},{4,5},{5,4},{6,7},{7,6},{8,9},{9,8},{10,11... | collective-permute-start | bytes 4030472 | tf_op jit(solution)/shard_map/ppermute | solution.py:86
  74.8 64.8 %copy-start.91 = (f32[768]{0:T(1024)}, f32[768]{0:T(1024)S(1)}, u32[]{:S(2)}) copy-start(f32[768]{0:T(1024)S(1)} %get-tuple-element.136) | copy-start | bytes 9220
  95.5 16.4 %collective-permute-start.17 = (bf16[2,1312,128]{2,1,0:T(8,128)(2,1)S(1)}, bf16[2,1312,128]{2,1,0:T(8,128)(2,1)S(1)}, u32[]{:S(2)}, u32[]{:S(2)}) collective-permute-start(bf16[2,1312,128]{2,1,0:T(8,128)(2,1)S(1)} %slice.228), channel_id=1, source_target_pairs={{0,2},{1,3},{2,0},{3,1},{4,6},{5,7},{6,4},{7,5},{8,10},{9,11},{10,... | collective-permute-start | bytes 2015240 | tf_op jit(solution)/shard_map/ppermute | solution.py:86
  98.2 16.1 %collective-permute-start.18 = (bf16[2,1312,128]{2,1,0:T(8,128)(2,1)S(1)}, bf16[2,1312,128]{2,1,0:T(8,128)(2,1)S(1)}, u32[]{:S(2)}, u32[]{:S(2)}) collective-permute-start(bf16[2,1312,128]{2,1,0:T(8,128)(2,1)S(1)} %slice.229), channel_id=1, source_target_pairs={{0,4},{1,5},{2,6},{3,7},{4,0},{5,1},{6,2},{7,3},{8,12},{9,13},{10,... | collective-permute-start | bytes 2015240 | tf_op jit(solution)/shard_map/ppermute | solution.py:86
  99.5 17.7 %collective-permute-start.20 = (bf16[4,1312,128]{2,1,0:T(8,128)(2,1)}, bf16[4,1312,128]{2,1,0:T(8,128)(2,1)S(1)}, u32[]{:S(2)}, u32[]{:S(2)}) collective-permute-start(bf16[4,1312,128]{2,1,0:T(8,128)(2,1)} %collective-permute-done.15.refs_1_), channel_id=1, source_target_pairs={{0,1},{1,0},{2,3},{3,2},{4,5},{5,4},{6,7},{7,6},{8,9},{9,8},{10,11... | collective-permute-start | bytes 4030472 | tf_op jit(solution)/shard_map/ppermute | solution.py:86
  99.6 17.7 %collective-permute-start.21 = (bf16[4,1312,128]{2,1,0:T(8,128)(2,1)}, bf16[4,1312,128]{2,1,0:T(8,128)(2,1)}, u32[]{:S(2)}, u32[]{:S(2)}) collective-permute-start(bf16[4,1312,128]{2,1,0:T(8,128)(2,1)} %collective-permute-done.16.refs_2_), channel_id=1, source_target_pairs={{0,1},{1,0},{2,3},{3,2},{4,5},{5,4},{6,7},{7,6},{8,9},{9,8},{10,11... | collective-permute-start | bytes 4030472 | tf_op jit(solution)/shard_map/ppermute | solution.py:86
  111.9 5.4 %collective-permute-start.22 = (bf16[2,1312,128]{2,1,0:T(8,128)(2,1)S(1)}, bf16[2,1312,128]{2,1,0:T(8,128)(2,1)S(1)}, u32[]{:S(2)}, u32[]{:S(2)}) collective-permute-start(bf16[2,1312,128]{2,1,0:T(8,128)(2,1)S(1)} %collective-permute-done.17.refs_3_), channel_id=1, source_target_pairs={{0,1},{1,0},{2,3},{3,2},{4,5},{5,4},{6,7},{7,6},{8,9},{9,8},{10,11... | collective-permute-start | bytes 2015240 | tf_op jit(solution)/shard_map/ppermute | solution.py:86
  114.3 4.3 %collective-permute-start.23 = (bf16[2,1312,128]{2,1,0:T(8,128)(2,1)S(1)}, bf16[2,1312,128]{2,1,0:T(8,128)(2,1)}, u32[]{:S(2)}, u32[]{:S(2)}) collective-permute-start(bf16[2,1312,128]{2,1,0:T(8,128)(2,1)S(1)} %collective-permute-done.18.refs_4_), channel_id=1, source_target_pairs={{0,1},{1,0},{2,3},{3,2},{4,5},{5,4},{6,7},{7,6},{8,9},{9,8},{10,11... | collective-permute-start | bytes 2015240 | tf_op jit(solution)/shard_map/ppermute | solution.py:86
  152.8 5.7 %collective-permute-start.26 = (bf16[16,768]{1,0:T(8,128)(2,1)S(1)}, bf16[16,768]{1,0:T(8,128)(2,1)S(1)}, u32[]{:S(2)}, u32[]{:S(2)}) collective-permute-start(bf16[16,768]{1,0:T(8,128)(2,1)S(1)} %multiply_convert_fusion.3), channel_id=1, source_target_pairs={{0,24},{1,25},{2,26},{3,27},{4,28},{5,29},{6,30},{7,31},{8,16},{9,... | collective-permute-start | bytes 73736 | tf_op jit(solution)/shard_map/ppermute | solution.py:86
  155.5 4.7 %collective-permute-start.25 = (bf16[16,768]{1,0:T(8,128)(2,1)S(1)}, bf16[16,768]{1,0:T(8,128)(2,1)S(1)}, u32[]{:S(2)}, u32[]{:S(2)}) collective-permute-start(bf16[16,768]{1,0:T(8,128)(2,1)S(1)} %multiply_convert_fusion.3), channel_id=1, source_target_pairs={{0,16},{1,17},{2,18},{3,19},{4,20},{5,21},{6,22},{7,23},{8,24},{9,... | collective-permute-start | bytes 73736 | tf_op jit(solution)/shard_map/ppermute | solution.py:86
  155.6 4.7 %collective-permute-start.24 = (bf16[16,768]{1,0:T(8,128)(2,1)S(1)}, bf16[16,768]{1,0:T(8,128)(2,1)S(1)}, u32[]{:S(2)}, u32[]{:S(2)}) collective-permute-start(bf16[16,768]{1,0:T(8,128)(2,1)S(1)} %multiply_convert_fusion.3), channel_id=1, source_target_pairs={{0,8},{1,9},{2,10},{3,11},{4,12},{5,13},{6,14},{7,15},{8,0},{9,1},... | collective-permute-start | bytes 73736 | tf_op jit(solution)/shard_map/ppermute | solution.py:86
  160.3 5.8 %collective-permute-start.29 = (bf16[4,16,768]{2,1,0:T(8,128)(2,1)S(1)}, bf16[4,16,768]{2,1,0:T(8,128)(2,1)S(1)}, u32[]{:S(2)}, u32[]{:S(2)}) collective-permute-start(bf16[4,16,768]{2,1,0:T(8,128)(2,1)S(1)} %get-tuple-element.200), channel_id=1, source_target_pairs={{0,6},{1,7},{2,4},{3,5},{4,2},{5,3},{6,0},{7,1},{8,14},{9,15},{10,... | collective-permute-start | bytes 294920 | tf_op jit(solution)/shard_map/ppermute | solution.py:86
  161.2 5.7 %collective-permute-start.28 = (bf16[4,16,768]{2,1,0:T(8,128)(2,1)S(1)}, bf16[4,16,768]{2,1,0:T(8,128)(2,1)S(1)}, u32[]{:S(2)}, u32[]{:S(2)}) collective-permute-start(bf16[4,16,768]{2,1,0:T(8,128)(2,1)S(1)} %get-tuple-element.200), channel_id=1, source_target_pairs={{0,4},{1,5},{2,6},{3,7},{4,0},{5,1},{6,2},{7,3},{8,12},{9,13},{10,... | collective-permute-start | bytes 294920 | tf_op jit(solution)/shard_map/ppermute | solution.py:86
  162.5 4.6 %collective-permute-start.27 = (bf16[4,16,768]{2,1,0:T(8,128)(2,1)S(1)}, bf16[4,16,768]{2,1,0:T(8,128)(2,1)S(1)}, u32[]{:S(2)}, u32[]{:S(2)}) collective-permute-start(bf16[4,16,768]{2,1,0:T(8,128)(2,1)S(1)} %get-tuple-element.200), channel_id=1, source_target_pairs={{0,2},{1,3},{2,0},{3,1},{4,6},{5,7},{6,4},{7,5},{8,10},{9,11},{10,... | collective-permute-start | bytes 294920 | tf_op jit(solution)/shard_map/ppermute | solution.py:86
  167.9 3.3 collective-permute-start.30
  223.1 13.1 %collective-permute-start.31 = (bf16[4,1312,128]{2,1,0:T(8,128)(2,1)}, bf16[4,1312,128]{2,1,0:T(8,128)(2,1)S(1)}, u32[]{:S(2)}, u32[]{:S(2)}) collective-permute-start(bf16[4,1312,128]{2,1,0:T(8,128)(2,1)} %get-tuple-element.88), channel_id=1, source_target_pairs={{0,1},{1,0},{2,3},{3,2},{4,5},{5,4},{6,7},{7,6},{8,9},{9,8},{10,11... | collective-permute-start | bytes 4030472 | tf_op jit(solution)/shard_map/ppermute | solution.py:86
  223.7 8.0 %collective-permute-start.34 = (bf16[2,1312,128]{2,1,0:T(8,128)(2,1)}, bf16[2,1312,128]{2,1,0:T(8,128)(2,1)}, u32[]{:S(2)}, u32[]{:S(2)}) collective-permute-start(bf16[2,1312,128]{2,1,0:T(8,128)(2,1)} %get-tuple-element.94), channel_id=1, source_target_pairs={{0,1},{1,0},{2,3},{3,2},{4,5},{5,4},{6,7},{7,6},{8,9},{9,8},{10,11... | collective-permute-start | bytes 2015240 | tf_op jit(solution)/shard_map/ppermute | solution.py:86
  223.8 10.3 %collective-permute-start.35 = (bf16[2,1312,128]{2,1,0:T(8,128)(2,1)}, bf16[2,1312,128]{2,1,0:T(8,128)(2,1)}, u32[]{:S(2)}, u32[]{:S(2)}) collective-permute-start(bf16[2,1312,128]{2,1,0:T(8,128)(2,1)} %get-tuple-element.96), channel_id=1, source_target_pairs={{0,1},{1,0},{2,3},{3,2},{4,5},{5,4},{6,7},{7,6},{8,9},{9,8},{10,11... | collective-permute-start | bytes 2015240 | tf_op jit(solution)/shard_map/ppermute | solution.py:86
  229.8 7.9 %collective-permute-start.32 = (bf16[4,1312,128]{2,1,0:T(8,128)(2,1)}, bf16[4,1312,128]{2,1,0:T(8,128)(2,1)}, u32[]{:S(2)}, u32[]{:S(2)}) collective-permute-start(bf16[4,1312,128]{2,1,0:T(8,128)(2,1)} %get-tuple-element.90), channel_id=1, source_target_pairs={{0,1},{1,0},{2,3},{3,2},{4,5},{5,4},{6,7},{7,6},{8,9},{9,8},{10,11... | collective-permute-start | bytes 4030472 | tf_op jit(solution)/shard_map/ppermute | solution.py:86
  230.1 10.5 %collective-permute-start.33 = (bf16[4,1312,128]{2,1,0:T(8,128)(2,1)}, bf16[4,1312,128]{2,1,0:T(8,128)(2,1)S(1)}, u32[]{:S(2)}, u32[]{:S(2)}) collective-permute-start(bf16[4,1312,128]{2,1,0:T(8,128)(2,1)} %get-tuple-element.92), channel_id=1, source_target_pairs={{0,1},{1,0},{2,3},{3,2},{4,5},{5,4},{6,7},{7,6},{8,9},{9,8},{10,11... | collective-permute-start | bytes 4030472 | tf_op jit(solution)/shard_map/ppermute | solution.py:86
  257.3 17.6 %collective-permute-start.36 = (bf16[2,1312,128]{2,1,0:T(8,128)(2,1)}, bf16[2,1312,128]{2,1,0:T(8,128)(2,1)}, u32[]{:S(2)}, u32[]{:S(2)}) collective-permute-start(bf16[2,1312,128]{2,1,0:T(8,128)(2,1)} %add_convert_fusion.7), channel_id=1, source_target_pairs={{0,2},{1,3},{2,0},{3,1},{4,6},{5,7},{6,4},{7,5},{8,10},{9,11},{10,... | collective-permute-start | bytes 2015240 | tf_op jit(solution)/shard_map/ppermute | solution.py:86
  258.7 17.3 %collective-permute-start.37 = (bf16[2,1312,128]{2,1,0:T(8,128)(2,1)}, bf16[2,1312,128]{2,1,0:T(8,128)(2,1)}, u32[]{:S(2)}, u32[]{:S(2)}) collective-permute-start(bf16[2,1312,128]{2,1,0:T(8,128)(2,1)} %add_convert_fusion.6), channel_id=1, source_target_pairs={{0,4},{1,5},{2,6},{3,7},{4,0},{5,1},{6,2},{7,3},{8,12},{9,13},{10,... | collective-permute-start | bytes 2015240 | tf_op jit(solution)/shard_map/ppermute | solution.py:86
  286.6 30.8 %collective-permute-start.38 = (bf16[4,1312,128]{2,1,0:T(8,128)(2,1)}, bf16[4,1312,128]{2,1,0:T(8,128)(2,1)S(1)}, u32[]{:S(2)}, u32[]{:S(2)}) collective-permute-start(bf16[4,1312,128]{2,1,0:T(8,128)(2,1)} %pad_maximum_fusion.2), channel_id=1, source_target_pairs={{0,2},{1,3},{2,0},{3,1},{4,6},{5,7},{6,4},{7,5},{8,10},{9,11},{10,... | collective-permute-start | bytes 4030472 | tf_op jit(solution)/shard_map/ppermute | solution.py:86
  289.7 30.8 %collective-permute-start.39 = (bf16[4,1312,128]{2,1,0:T(8,128)(2,1)}, bf16[4,1312,128]{2,1,0:T(8,128)(2,1)}, u32[]{:S(2)}, u32[]{:S(2)}) collective-permute-start(bf16[4,1312,128]{2,1,0:T(8,128)(2,1)} %pad_maximum_fusion.3), channel_id=1, source_target_pairs={{0,4},{1,5},{2,6},{3,7},{4,0},{5,1},{6,2},{7,3},{8,12},{9,13},{10,... | collective-permute-start | bytes 4030472 | tf_op jit(solution)/shard_map/ppermute | solution.py:86
  320.6 6.2 %collective-permute-start.45 = (bf16[4,624,128]{2,1,0:T(8,128)(2,1)}, bf16[4,624,128]{2,1,0:T(8,128)(2,1)S(1)}, u32[]{:S(2)}, u32[]{:S(2)}) collective-permute-start(bf16[4,624,128]{2,1,0:T(8,128)(2,1)} %get-tuple-element.122), channel_id=1, source_target_pairs={{0,1},{1,0},{2,3},{3,2},{4,5},{5,4},{6,7},{7,6},{8,9},{9,8},{10,11... | collective-permute-start | bytes 1916936 | tf_op jit(solution)/shard_map/ppermute | solution.py:86
  320.6 3.1 collective-permute-start.46
  321.1 4.4 %collective-permute-start.42 = (bf16[2,624,128]{2,1,0:T(8,128)(2,1)}, bf16[2,624,128]{2,1,0:T(8,128)(2,1)S(1)}, u32[]{:S(2)}, u32[]{:S(2)}) collective-permute-start(bf16[2,624,128]{2,1,0:T(8,128)(2,1)} %get-tuple-element.120), channel_id=1, source_target_pairs={{0,1},{1,0},{2,3},{3,2},{4,5},{5,4},{6,7},{7,6},{8,9},{9,8},{10,11... | collective-permute-start | bytes 958472 | tf_op jit(solution)/shard_map/ppermute | solution.py:86
  321.1 7.1 %collective-permute-start.41 = (bf16[4,624,128]{2,1,0:T(8,128)(2,1)}, bf16[4,624,128]{2,1,0:T(8,128)(2,1)S(1)}, u32[]{:S(2)}, u32[]{:S(2)}) collective-permute-start(bf16[4,624,128]{2,1,0:T(8,128)(2,1)} %get-tuple-element.118), channel_id=1, source_target_pairs={{0,1},{1,0},{2,3},{3,2},{4,5},{5,4},{6,7},{7,6},{8,9},{9,8},{10,11... | collective-permute-start | bytes 1916936 | tf_op jit(solution)/shard_map/ppermute | solution.py:86
  321.6 34.6 %collective-permute-start.40 = (bf16[4,624,128]{2,1,0:T(8,128)(2,1)}, bf16[4,624,128]{2,1,0:T(8,128)(2,1)S(1)}, u32[]{:S(2)}, u32[]{:S(2)}) collective-permute-start(bf16[4,624,128]{2,1,0:T(8,128)(2,1)} %get-tuple-element.116), channel_id=1, source_target_pairs={{0,1},{1,0},{2,3},{3,2},{4,5},{5,4},{6,7},{7,6},{8,9},{9,8},{10,11... | collective-permute-start | bytes 1916936 | tf_op jit(solution)/shard_map/ppermute | solution.py:86
  323.7 22.7 %collective-permute-start.54 = (bf16[1312,128]{1,0:T(8,128)(2,1)S(1)}, bf16[1312,128]{1,0:T(8,128)(2,1)S(1)}, u32[]{:S(2)}, u32[]{:S(2)}) collective-permute-start(bf16[1312,128]{1,0:T(8,128)(2,1)S(1)} %get-tuple-element.190), channel_id=1, source_target_pairs={{0,24},{1,25},{2,26},{3,27},{4,28},{5,29},{6,30},{7,31},{8,16},{9,... | collective-permute-start | bytes 1007624 | tf_op jit(solution)/shard_map/ppermute | solution.py:86
  325.5 30.4 %collective-permute-start.53 = (bf16[1312,128]{1,0:T(8,128)(2,1)S(1)}, bf16[1312,128]{1,0:T(8,128)(2,1)S(1)}, u32[]{:S(2)}, u32[]{:S(2)}) collective-permute-start(bf16[1312,128]{1,0:T(8,128)(2,1)S(1)} %get-tuple-element.191), channel_id=1, source_target_pairs={{0,16},{1,17},{2,18},{3,19},{4,20},{5,21},{6,22},{7,23},{8,24},{9,... | collective-permute-start | bytes 1007624 | tf_op jit(solution)/shard_map/ppermute | solution.py:86
  326.8 9.7 %collective-permute-start.47 = (bf16[2,624,128]{2,1,0:T(8,128)(2,1)S(1)}, bf16[2,624,128]{2,1,0:T(8,128)(2,1)S(1)}, u32[]{:S(2)}, u32[]{:S(2)}) collective-permute-start(bf16[2,624,128]{2,1,0:T(8,128)(2,1)S(1)} %add_convert_fusion.13), channel_id=1, source_target_pairs={{0,2},{1,3},{2,0},{3,1},{4,6},{5,7},{6,4},{7,5},{8,10},{9,11},{10,... | collective-permute-start | bytes 958472 | tf_op jit(solution)/shard_map/ppermute | solution.py:86
  328.2 27.7 %collective-permute-start.52 = (bf16[1312,128]{1,0:T(8,128)(2,1)S(1)}, bf16[1312,128]{1,0:T(8,128)(2,1)S(1)}, u32[]{:S(2)}, u32[]{:S(2)}) collective-permute-start(bf16[1312,128]{1,0:T(8,128)(2,1)S(1)} %get-tuple-element.189), channel_id=1, source_target_pairs={{0,8},{1,9},{2,10},{3,11},{4,12},{5,13},{6,14},{7,15},{8,0},{9,1},... | collective-permute-start | bytes 1007624 | tf_op jit(solution)/shard_map/ppermute | solution.py:86
  336.6 8.8 %collective-permute-start.43 = (bf16[2,624,128]{2,1,0:T(8,128)(2,1)S(1)}, bf16[2,624,128]{2,1,0:T(8,128)(2,1)S(1)}, u32[]{:S(2)}, u32[]{:S(2)}) collective-permute-start(bf16[2,624,128]{2,1,0:T(8,128)(2,1)S(1)} %add_convert_fusion.15), channel_id=1, source_target_pairs={{0,4},{1,5},{2,6},{3,7},{4,0},{5,1},{6,2},{7,3},{8,12},{9,13},{10,... | collective-permute-start | bytes 958472 | tf_op jit(solution)/shard_map/ppermute | solution.py:86
  345.4 14.8 %collective-permute-start.48 = (bf16[4,624,128]{2,1,0:T(8,128)(2,1)S(1)}, bf16[4,624,128]{2,1,0:T(8,128)(2,1)S(1)}, u32[]{:S(2)}, u32[]{:S(2)}) collective-permute-start(bf16[4,624,128]{2,1,0:T(8,128)(2,1)S(1)} %pad_maximum_fusion.6), channel_id=1, source_target_pairs={{0,4},{1,5},{2,6},{3,7},{4,0},{5,1},{6,2},{7,3},{8,12},{9,13},{10,... | collective-permute-start | bytes 1916936 | tf_op jit(solution)/shard_map/ppermute | solution.py:86
  346.4 14.6 %collective-permute-start.44 = (bf16[4,624,128]{2,1,0:T(8,128)(2,1)S(1)}, bf16[4,624,128]{2,1,0:T(8,128)(2,1)S(1)}, u32[]{:S(2)}, u32[]{:S(2)}) collective-permute-start(bf16[4,624,128]{2,1,0:T(8,128)(2,1)S(1)} %pad_maximum_fusion.5), channel_id=1, source_target_pairs={{0,2},{1,3},{2,0},{3,1},{4,6},{5,7},{6,4},{7,5},{8,10},{9,11},{10,... | collective-permute-start | bytes 1916936 | tf_op jit(solution)/shard_map/ppermute | solution.py:86
  361.3 7.3 %collective-permute-start.51 = (bf16[624,128]{1,0:T(8,128)(2,1)S(1)}, bf16[624,128]{1,0:T(8,128)(2,1)S(1)}, u32[]{:S(2)}, u32[]{:S(2)}) collective-permute-start(bf16[624,128]{1,0:T(8,128)(2,1)S(1)} %get-tuple-element.194), channel_id=1, source_target_pairs={{0,24},{1,25},{2,26},{3,27},{4,28},{5,29},{6,30},{7,31},{8,16},{9,... | collective-permute-start | bytes 479240 | tf_op jit(solution)/shard_map/ppermute | solution.py:86
  362.6 15.7 %collective-permute-start.50 = (bf16[624,128]{1,0:T(8,128)(2,1)S(1)}, bf16[624,128]{1,0:T(8,128)(2,1)S(1)}, u32[]{:S(2)}, u32[]{:S(2)}) collective-permute-start(bf16[624,128]{1,0:T(8,128)(2,1)S(1)} %get-tuple-element.195), channel_id=1, source_target_pairs={{0,16},{1,17},{2,18},{3,19},{4,20},{5,21},{6,22},{7,23},{8,24},{9,... | collective-permute-start | bytes 479240 | tf_op jit(solution)/shard_map/ppermute | solution.py:86
  367.3 11.1 %collective-permute-start.49 = (bf16[624,128]{1,0:T(8,128)(2,1)S(1)}, bf16[624,128]{1,0:T(8,128)(2,1)S(1)}, u32[]{:S(2)}, u32[]{:S(2)}) collective-permute-start(bf16[624,128]{1,0:T(8,128)(2,1)S(1)} %get-tuple-element.193), channel_id=1, source_target_pairs={{0,8},{1,9},{2,10},{3,11},{4,12},{5,13},{6,14},{7,15},{8,0},{9,1},... | collective-permute-start | bytes 479240 | tf_op jit(solution)/shard_map/ppermute | solution.py:86
  380.7 1.3 collective-permute-start.55
  382.6 7.4 %collective-permute-start.56 = (f32[]{:T(128)}, f32[]{:T(128)}, u32[]{:S(2)}, u32[]{:S(2)}) collective-permute-start(f32[]{:T(128)} %add.525), channel_id=1, source_target_pairs={{0,2},{1,3},{2,0},{3,1},{4,6},{5,7},{6,4},{7,5},{8,10},{9,11},{10,... | collective-permute-start | bytes 20 | tf_op jit(solution)/shard_map/ppermute | solution.py:86
  385.1 5.5 %collective-permute-start.57 = (f32[]{:T(128)}, f32[]{:T(128)}, u32[]{:S(2)}, u32[]{:S(2)}) collective-permute-start(f32[]{:T(128)} %add.525), channel_id=1, source_target_pairs={{0,4},{1,5},{2,6},{3,7},{4,0},{5,1},{6,2},{7,3},{8,12},{9,13},{10,... | collective-permute-start | bytes 20 | tf_op jit(solution)/shard_map/ppermute | solution.py:86
  387.1 4.4 %collective-permute-start.58 = (f32[]{:T(128)}, f32[]{:T(128)}, u32[]{:S(2)}, u32[]{:S(2)}) collective-permute-start(f32[]{:T(128)} %add.525), channel_id=1, source_target_pairs={{0,6},{1,7},{2,4},{3,5},{4,2},{5,3},{6,0},{7,1},{8,14},{9,15},{10,... | collective-permute-start | bytes 20 | tf_op jit(solution)/shard_map/ppermute | solution.py:86
  392.9 8.3 %collective-permute-start.59 = (f32[]{:T(128)}, f32[]{:T(128)}, u32[]{:S(2)}, u32[]{:S(2)}) collective-permute-start(f32[]{:T(128)} %add.528), channel_id=1, source_target_pairs={{0,8},{1,9},{2,10},{3,11},{4,12},{5,13},{6,14},{7,15},{8,0},{9,1},... | collective-permute-start | bytes 20 | tf_op jit(solution)/shard_map/ppermute | solution.py:86
  394.3 7.5 %collective-permute-start.60 = (f32[]{:T(128)}, f32[]{:T(128)}, u32[]{:S(2)}, u32[]{:S(2)}) collective-permute-start(f32[]{:T(128)} %add.528), channel_id=1, source_target_pairs={{0,16},{1,17},{2,18},{3,19},{4,20},{5,21},{6,22},{7,23},{8,24},{9,... | collective-permute-start | bytes 20 | tf_op jit(solution)/shard_map/ppermute | solution.py:86
  398.2 5.3 %collective-permute-start.61 = (f32[]{:T(128)}, f32[]{:T(128)}, u32[]{:S(2)}, u32[]{:S(2)}) collective-permute-start(f32[]{:T(128)} %add.528), channel_id=1, source_target_pairs={{0,24},{1,25},{2,26},{3,27},{4,28},{5,29},{6,30},{7,31},{8,16},{9,... | collective-permute-start | bytes 20 | tf_op jit(solution)/shard_map/ppermute | solution.py:86
  (106 other events, 751.8 us)
